TPU v7x, 128 devices: a whole 4x4x4 slice. The times are simulated.
128 devices in a mesh: gz: 32 (over y, z, core), gy: 4 (over x).
Axes of the slice: x: 4, y: 4, z: 4, core: 2. Of those that a mesh axis runs over, the one named last changes fastest.
Arguments:
- features: bfloat16 [1024, 64, 512], P(('gz', 'gy')), may hold values from -6 to 6
- occupancy: int32 [1024, 512], P(('gz', 'gy')), may hold values from 0 to 1, as said below
- neighbors: int32 [1024, 27], P(('gz', 'gy')), may hold values from -1 to 1023, as said below
- coarse_dest: int32 [1024], P(('gz', 'gy')), may hold values from -1 to 8191, as said below
- w_sub: bfloat16 [27, 64, 64], replicated, may hold values from -0.15625 to 0.15625
- w_down: bfloat16 [8, 128, 64], replicated, may hold values from -0.25 to 0.25
- coarse_grad: bfloat16 [1024, 128, 512], P(('gz', 'gy')), may hold values from -6 to 6
Outputs:
- coarse: bfloat16 [1024, 128, 512], P(('gz', 'gy'))
- feat_grad: bfloat16 [1024, 64, 512], P(('gz', 'gy'))
- w_sub_grad: float32 [27, 64, 64], replicated
- w_down_grad: float32 [8, 128, 64], replicated
Inputs may be any that keep to these rules, and one draw needn't show every extreme that they name: `neighbors`: slot s of tile slot index t = d * 8 + s lies on device d = gz index * 4 + gy index. Tiles sit on a grid, each device's region being 2 x 4 x 8 tile positions; its active tiles fill slots 0 upward, the rest are -1 everywhere. An entry is another tile's slot only if that tile is the geometric neighbor, which lies on the same device or on a device whose gz index differs by the z displacement and whose gy index differs by the y displacement (never both by wrapping); the table is symmetric. Some device fills all 8 slots. `occupancy`: 0 on slots without a tile. `coarse_dest`: entries of tiles are distinct; the coarse tile c lies on device c // 8, which is the slot's own device or the one whose gz index differs only in its lowest bit, with the same gy index.
All inputs are finite; a program needn't handle non-finite values.
Results may differ from a plain program's by a relative error of at most 0.005.
The roundings to bfloat16 on the way count: a program that leaves them out, or rounds other values in their place, can miss the bound.
Values may be sent and summed in bfloat16 or wider, within the bound.
A program may use at most 192 MiB of HBM per device.

v0:
```python
import jax
import jax.numpy as jnp
from jax import lax
from jax.sharding import PartitionSpec as P


def padded_2(block, sides, width):
    for axis, dim in sides:
        count = lax.axis_size(axis)
        forward = [(i, i + 1) for i in range(count - 1)]
        backward = [(target, source) for source, target in forward]
        low = lax.ppermute(
            lax.slice_in_dim(block, block.shape[dim] - width, None, axis=dim), axis, forward
        )
        high = lax.ppermute(lax.slice_in_dim(block, 0, width, axis=dim), axis, backward)
        block = jnp.concatenate([low, block, high], axis=dim)
    return block


def from_partner(block, axis, bit):
    count = lax.axis_size(axis)
    route = []
    for low in range(count):
        high = low | 1 << bit
        if high != low and high < count:
            route += [(low, high), (high, low)]
    return lax.ppermute(block, axis, route)


def rim_ranges(index):
    if index == 0:
        return (slice(7, 8), slice(0, 1))
    if index == 1:
        return (slice(0, 8), slice(1, 9))
    return (slice(0, 1), slice(9, 10))


def expand_rows(flags):
    return flags[:, None, None, None, None]


def build_padded(field5, link_parts):
    present, slot_of, shift_z, shift_y = link_parts
    rows, channels = (field5.shape[0], field5.shape[1])
    z_source = jnp.stack([field5[:, :, 0], field5[:, :, 7]]).reshape(2, rows, channels * 64)
    z_faces = padded_2(z_source, (("gz", 0),), 1).reshape(4, rows, channels, 8, 8)
    y_source = jnp.stack([field5[:, :, :, 0], field5[:, :, :, 7]]).reshape(2, rows, channels * 64)
    y_faces = padded_2(y_source, (("gy", 0),), 1).reshape(4, rows, channels, 8, 8)
    edge_source = jnp.stack(
        [
            jnp.stack([field5[:, :, 0, 0], field5[:, :, 0, 7]]),
            jnp.stack([field5[:, :, 7, 0], field5[:, :, 7, 7]]),
        ]
    ).reshape(2, 2, rows, channels * 8)
    edge_all = padded_2(edge_source, (("gz", 0), ("gy", 1)), 1)
    edge_all = edge_all.reshape(4, 4, rows, channels, 8)
    local_flag = present & (shift_z == 0) & (shift_y == 0)
    nearby = field5[slot_of]
    nearby = jnp.where(local_flag[:, :, None, None, None, None], nearby, jnp.zeros_like(nearby))
    padded = jnp.zeros((rows, channels, 10, 10, 10), field5.dtype)
    for a in range(3):
        for b in range(3):
            for c in range(3):
                column = 9 * a + 3 * b + c
                from_z, into_z = rim_ranges(a)
                from_y, into_y = rim_ranges(b)
                from_x, into_x = rim_ranges(c)
                chosen = slot_of[:, column]
                live = present[:, column]
                step_z = shift_z[:, column]
                step_y = shift_y[:, column]
                if a == 1 and b == 1 and (c == 1):
                    portion = jnp.where(
                        expand_rows(local_flag[:, column]), field5, jnp.zeros_like(field5)
                    )
                else:
                    portion = nearby[:, column][:, :, from_z, from_y, from_x]
                side_z = 0 if a == 0 else 3
                side_y = 0 if b == 0 else 3
                if a != 1:
                    remote = z_faces[side_z][:, :, from_y, from_x][chosen][:, :, None]
                    portion = jnp.where(
                        expand_rows(live & (step_z == a - 1) & (step_y == 0)), remote, portion
                    )
                if b != 1:
                    remote = y_faces[side_y][:, :, from_z, from_x][chosen][:, :, :, None]
                    portion = jnp.where(
                        expand_rows(live & (step_z == 0) & (step_y == b - 1)), remote, portion
                    )
                if a != 1 and b != 1:
                    remote = edge_all[side_z, side_y][:, :, from_x][chosen][:, :, None, None]
                    portion = jnp.where(
                        expand_rows(live & (step_z == a - 1) & (step_y == b - 1)), remote, portion
                    )
                padded = padded.at[:, :, into_z, into_y, into_x].set(portion)
    return padded


def conv_apply(padded, kernel):
    rows, channels = (padded.shape[0], kernel.shape[0])
    result = lax.conv_general_dilated(
        padded,
        kernel,
        (1, 1, 1),
        "VALID",
        dimension_numbers=("NCDHW", "OIDHW", "NCDHW"),
        preferred_element_type=jnp.float32,
    )
    return result.reshape(rows, channels, 512)


def kernel_grad(padded, pre_grad5):
    result = lax.conv_general_dilated(
        padded,
        pre_grad5,
        (1, 1, 1),
        "VALID",
        dimension_numbers=("CNDHW", "IODHW", "NCDHW"),
        preferred_element_type=jnp.float32,
    )
    inputs_now, outputs_now = (result.shape[0], result.shape[1])
    return result.transpose(2, 3, 4, 1, 0).reshape(27, outputs_now, inputs_now)


def split_phases(field):
    rows, channels = (field.shape[0], field.shape[1])
    field = field.reshape(rows, channels, 4, 2, 4, 2, 4, 2).transpose(0, 3, 5, 7, 1, 2, 4, 6)
    return field.reshape(rows, 8, channels, 64)


def merge_phases(field):
    rows, channels = (field.shape[0], field.shape[2])
    field = field.reshape(rows, 2, 2, 2, channels, 4, 4, 4).transpose(0, 4, 5, 1, 6, 2, 7, 3)
    return field.reshape(rows, channels, 512)


def place_blocks(blocks, dest, self_index, slot_span):
    owned = (dest >= 0) & (dest // slot_span == self_index)
    index = jnp.where(owned, dest - self_index * slot_span, slot_span)
    flat = (
        jnp.zeros((slot_span, blocks.shape[1], 64), jnp.bfloat16).at[index].set(blocks, mode="drop")
    )
    tiles_now = slot_span // 8
    outer = flat.reshape(tiles_now, 2, 2, 2, blocks.shape[1], 4, 4, 4).transpose(
        0, 4, 1, 5, 2, 6, 3, 7
    )
    return outer.reshape(tiles_now, blocks.shape[1], 512)


def fetch_blocks(grad_blocks, dest, self_index, slot_span):
    owned = (dest >= 0) & (dest // slot_span == self_index)
    chosen = grad_blocks[jnp.where(owned, dest - self_index * slot_span, 0)]
    return jnp.where(owned[:, None, None], chosen, jnp.zeros_like(chosen))


def shards(features, occupancy, neighbors, coarse_dest, w_sub, w_down, coarse_grad):
    rows, channels = (features.shape[0], features.shape[1])
    out_channels = w_down.shape[1]
    strips_now = lax.axis_size("gy")
    devices_now = lax.axis_size("gz") * strips_now
    self_index = lax.axis_index("gz") * strips_now + lax.axis_index("gy")
    slot_span = coarse_grad.shape[0] * 8
    occupied = occupancy.astype(jnp.float32)[:, None, :]
    masked = features * occupancy.astype(jnp.bfloat16)[:, None, :]
    owner_device = jnp.floor_divide(neighbors, rows)
    link_parts = (
        neighbors >= 0,
        jnp.where(neighbors >= 0, neighbors % rows, 0),
        owner_device // strips_now - lax.axis_index("gz"),
        owner_device % strips_now - lax.axis_index("gy"),
    )
    weights5 = w_sub.reshape(3, 3, 3, channels, channels)
    forward_kernel = weights5.transpose(3, 4, 0, 1, 2)
    backward_kernel = weights5[::-1, ::-1, ::-1].transpose(4, 3, 0, 1, 2)
    x_padded = build_padded(masked.reshape(rows, channels, 8, 8, 8), link_parts)
    preact = conv_apply(x_padded, forward_kernel)
    activated = (jax.nn.silu(preact) * occupied).astype(jnp.bfloat16)
    own_slots = (coarse_dest >= 0) & (coarse_dest // slot_span == self_index)
    inner = coarse_grad.reshape(coarse_grad.shape[0], out_channels, 2, 4, 2, 4, 2, 4).transpose(
        0, 2, 4, 6, 1, 3, 5, 7
    )
    grad_blocks = inner.reshape(slot_span, out_channels, 64)
    moved_act, moved_dest = from_partner((activated, coarse_dest), "gz", 0)
    both_dest = jnp.concatenate([coarse_dest, moved_dest])
    phases = split_phases(jnp.concatenate([activated, moved_act]))
    blocks = jnp.einsum("koi,tkiv->tov", w_down, phases, preferred_element_type=jnp.float32).astype(
        jnp.bfloat16
    )
    coarse = place_blocks(blocks, both_dest, self_index, slot_span)
    out_grad = fetch_blocks(grad_blocks, both_dest, self_index, slot_span)
    act_all = merge_phases(
        jnp.einsum("koi,tov->tkiv", w_down, out_grad, preferred_element_type=jnp.float32)
    ).astype(jnp.bfloat16)
    w_down_part = jnp.einsum("tov,tkiv->koi", out_grad, phases, preferred_element_type=jnp.float32)
    act_back = from_partner(act_all[rows:], "gz", 0)
    act_grad = jnp.where(own_slots[:, None, None], act_all[:rows], act_back)
    sigma = jax.nn.sigmoid(preact)
    pre_grad = (
        act_grad.astype(jnp.float32) * sigma * (1.0 + preact * (1.0 - sigma)) * occupied
    ).astype(jnp.bfloat16)
    pre_grad5 = pre_grad.reshape(rows, channels, 8, 8, 8)
    grad_padded = build_padded(pre_grad5, link_parts)
    feat_grad = (conv_apply(grad_padded, backward_kernel) * occupied).astype(jnp.bfloat16)
    w_sub_part = kernel_grad(x_padded, pre_grad5)
    w_sub_sum, w_down_sum = lax.psum((w_sub_part, w_down_part), ("gz", "gy"))
    scale = (rows * devices_now * 512.0) ** (-0.5)
    return (coarse, feat_grad, w_sub_sum * scale, w_down_sum * scale)


def solution(mesh):
    return jax.shard_map(
        shards,
        mesh=mesh,
        in_specs=(
            P(("gz", "gy"), None, None),
            P(("gz", "gy"), None),
            P(("gz", "gy"), None),
            P(("gz", "gy")),
            P(),
            P(),
            P(("gz", "gy"), None, None),
        ),
        out_specs=(P(("gz", "gy"), None, None), P(("gz", "gy"), None, None), P(), P()),
        check_vma=False,
    )
```

profile of v0, /device:TPU:1, one launch (start us, length us, event | category | flops | bytes accessed | tf_op | source)
XLA Modules:
  0.0 747.0 jit_solution(4438274659426660074)
XLA Ops:
  12.5 4.9 collective-permute-start.1
  19.2 1.9 collective-permute-start.2
  22.4 2.1 slice.3379
  24.6 3.7 collective-permute-start.5
  29.6 2.1 slice.3382
  31.6 3.9 collective-permute-start.6
  44.5 11.7 %gather_fusion.3 = bf16[216,64,8,8,8]{1,4,3,2,0:T(8,128)(2,1)} fusion(bf16[8,64,8,8,8]{1,4,3,2,0:T(8,128)(2,1)S(1)} %bitcast.586, s32[1024]{0:T(1024)S(1)} %get-tuple-element.984), kind=kCustom, calls=%fused_computation.3 | custom fusion | bytes 28312416 | tf_op jit(solution)/shard_map/gather | solution.py:58
  56.3 25.9 %copy_select_fusion.1 = bf16[8,27,64,8,8,8]{2,0,5,4,3,1:T(8,128)(2,1)} fusion(bf16[8,27,64,8,8,8]{2,5,4,3,1,0:T(8,128)(2,1)} %bitcast.588, pred[8,27]{0,1:T(8,128)(4,1)S(1)} %copy.204), kind=kLoop, calls=%fused_computation.101 | loop fusion | flops 7077888 | bytes 28311768 | tf_op jit(solution)/shard_map/jit(_where)/select_n | solution.py:59
  82.2 6.8 slice_bitcast_fusion.45
  89.0 15.0 %slice_bitcast_fusion.26 = (bf16[8,64,8,8,8]{1,0,4,3,2:T(8,128)(2,1)}, bf16[8,64,8,8,8]{1,0,4,3,2:T(8,128)(2,1)}, bf16[8,64,8,8,8]{1,0,4,3,2:T(8,128)(2,1)}, bf1...) fusion(bf16[8,27,64,8,8,8]{2,0,5,4,3,1:T(8,128)(2,1)} %copy_sel, ...), kind=kLoop, calls=%fused_computation.149 | loop fusion | bytes 19922944 | tf_op jit(solution)/shard_map/squeeze | solution.py:77
  105.2 2.1 slice.3430
  125.2 13.6 %collective-permute-start.7 = (bf16[1,8,4096]{2,1,0:T(8,128)(2,1)}, bf16[1,8,4096]{2,1,0:T(8,128)(2,1)}, u32[]{:S(2)}, u32[]{:S(2)}) collective-permute-start(bf16[1,8,4096]{2,1,0:T(8,128)(2,1)} %slice.3430), channel_id=1, source_target_pairs={{1,0},{2,1},{3,2},{5,4},{6,5},{7,6},{9,8},{10,9},{11,10},{13,12},{... | collective-permute-start | bytes 196616 | tf_op jit(solution)/shard_map/ppermute | solution.py:15
  142.4 2.4 copy.501
  147.2 4.0 collective-permute-start.3
  155.3 3.0 collective-permute-start.8
  159.1 2.5 reshape.3803
  178.4 2.1 squeeze.137
  180.4 1.8 fusion.191
  183.5 2.1 squeeze.138
  185.6 1.8 fusion.196
  192.1 3.1 squeeze.146
  195.2 4.9 fusion.186
  206.0 2.1 squeeze.159
  208.1 2.2 fusion.187
  226.3 2.0 copy.378
  241.9 1.9 copy.386
  244.5 1.9 copy.388
  246.5 2.0 copy.389
  259.7 1.9 copy.397
  318.6 11.0 %fusion.204 = f32[8,64,8,8,8]{1,0,4,3,2:T(8,128)} fusion(bf16[8,64,10,10,10]{1,0,4,3,2:T(8,128)(2,1)} %constant_dynamic-update-slice_fusion.15, bf16[3,3,3,64,64]{4,3,2,1,0:T(8,128)(2,1)S(1)} %bitcast.584), kind=kOutput, calls=%fused_computation.642 | convolution fusion | flops 905969664 | bytes 2293760 | tf_op jit(solution)/shard_map/conv_general_dilated | solution.py:101
  329.5 1.9 copy.283
  331.5 3.4 fusion.9
  334.9 5.4 fusion.206
  341.2 11.9 %gather_fusion.53 = bf16[216,64,8,8,8]{1,4,3,2,0:T(8,128)(2,1)} fusion(bf16[8,64,8,8,8]{1,4,3,2,0:T(8,128)(2,1)S(1)} %copy.293, s32[1024]{0:T(1024)S(1)} %copy-done.59), kind=kCustom, calls=%fused_computation.53 | custom fusion | bytes 28312416 | tf_op jit(solution)/shard_map/gather | solution.py:58
  353.1 25.9 %copy_select_fusion = bf16[8,27,64,8,8,8]{2,0,5,4,3,1:T(8,128)(2,1)} fusion(bf16[8,27,64,8,8,8]{2,5,4,3,1,0:T(8,128)(2,1)} %bitcast.587, pred[8,27]{0,1:T(8,128)(4,1)S(1)} %copy-done.57), kind=kLoop, calls=%fused_computation.100 | loop fusion | flops 7077888 | bytes 28311768 | tf_op jit(solution)/shard_map/jit(_where)/select_n | solution.py:59
  379.0 6.9 slice_bitcast_fusion.19
  385.9 15.0 %slice_bitcast_fusion = (bf16[8,64,8,8,8]{1,0,4,3,2:T(8,128)(2,1)}, bf16[8,64,8,8,8]{1,0,4,3,2:T(8,128)(2,1)}, bf16[8,64,8,8,8]{1,0,4,3,2:T(8,128)(2,1)}, bf16[8...) fusion(bf16[8,27,64,8,8,8]{2,0,5,4,3,1:T(8,128)(2,1)} %copy_sel, ...), kind=kLoop, calls=%fused_computation.123 | loop fusion | bytes 19922944 | tf_op jit(solution)/shard_map/squeeze | solution.py:77
  401.6 3.5 collective-permute-start.11
  405.9 1.9 collective-permute-start.12
  407.8 3.1 collective-permute-done.12
  410.9 4.3 collective-permute-start.13
  418.7 2.1 slice.3586
  420.7 4.6 collective-permute-start.15
  425.9 2.1 slice.3589
  428.0 4.0 collective-permute-start.16
  432.6 2.1 slice.3613
  438.1 1.9 collective-permute-start.18
  440.0 2.6 reshape.3813
  453.7 2.1 squeeze.171
  455.8 1.8 fusion.176
  458.9 2.1 squeeze.172
  467.5 3.1 squeeze.180
  470.6 4.5 fusion.171
  481.0 2.1 squeeze.193
  483.1 2.1 fusion.172
  502.3 2.0 copy.414
  535.6 2.0 copy.424
  546.8 1.9 copy.433
  571.8 5.6 fusion.205
  577.4 1.9 copy.276
  582.5 2.7 fusion
  585.2 2.6 copy.365
  592.5 143.4 %all-reduce.5.cloned.1.call-done = (f32[27,64,64]{2,1,0:T(8,128)}, f32[8,128,64]{1,2,0:T(8,128)}) async-done(((f32[27,64,64]{2,1,0:T(8,128)}, f32[8,128,64]{1,2,0:T(8,128)}), (f32[27,64,64]{2,1,0:T(8,128)}, f32[8,128,64]{1,2,0:T(8,128)})) %all-reduce.5.cloned.1.call-update) | async-done | bytes 704528 | tf_op jit(solution)/shard_map/psum | solution.py:205
  735.8 2.2 broadcast_multiply_fusion
  (810 shorter events, 297.9 us)
Async XLA Ops:
  7.2 311.4 %copy-start = (bf16[27,64,64]{2,1,0:T(8,128)(2,1)S(1)}, bf16[27,64,64]{2,1,0:T(8,128)(2,1)}, u32[]{:S(2)}) copy-start(bf16[27,64,64]{2,1,0:T(8,128)(2,1)} %param.119) | copy-start | bytes 663556
  7.2 728.6 %all-reduce.5.cloned.1.call-start = ((), (), s32[]{:S(2)}) async-start(), calls=%async_computation | async-start | bytes 2293760 | tf_op jit(solution)/shard_map/psum | solution.py:205
  10.5 17.8 %copy-start.8 = (bf16[8,64,512]{1,0,2:T(8,128)(2,1)}, bf16[8,64,512]{1,0,2:T(8,128)(2,1)S(1)}, u32[]{:S(2)}) copy-start(bf16[8,64,512]{1,0,2:T(8,128)(2,1)S(1)} %copy.194) | copy-start | bytes 1572868
  12.5 134.0 %collective-permute-start.1 = (bf16[1,2,8,512]{3,2,1,0:T(8,128)(2,1)}, bf16[1,2,8,512]{3,2,1,0:T(8,128)(2,1)}, u32[]{:S(2)}, u32[]{:S(2)}) collective-permute-start(bf16[1,2,8,512]{3,2,1,0:T(8,128)(2,1)} %constant_dynamic-update-slice_fusion), channel_id=1, source_target_pairs={{0,4},{4,8},{8,12},{12,16},{16,20},{20,24},{24,28},{28,32},{32,36}... | collective-permute-start | bytes 49160 | tf_op jit(solution)/shard_map/ppermute | solution.py:12
  19.2 127.2 %collective-permute-start.2 = (bf16[1,2,8,512]{3,2,1,0:T(8,128)(2,1)}, bf16[1,2,8,512]{3,2,1,0:T(8,128)(2,1)}, u32[]{:S(2)}, u32[]{:S(2)}) collective-permute-start(bf16[1,2,8,512]{3,2,1,0:T(8,128)(2,1)} %constant_dynamic-update-slice_fusion.2), channel_id=1, source_target_pairs={{4,0},{8,4},{12,8},{16,12},{20,16},{24,20},{28,24},{32,28},{36,32}... | collective-permute-start | bytes 49160 | tf_op jit(solution)/shard_map/ppermute | solution.py:15
  24.6 153.8 %collective-permute-start.5 = (bf16[1,8,4096]{2,1,0:T(8,128)(2,1)}, bf16[1,8,4096]{2,1,0:T(8,128)(2,1)}, u32[]{:S(2)}, u32[]{:S(2)}) collective-permute-start(bf16[1,8,4096]{2,1,0:T(8,128)(2,1)} %slice.3379), channel_id=1, source_target_pairs={{0,1},{1,2},{2,3},{4,5},{5,6},{6,7},{8,9},{9,10},{10,11},{12,13},{... | collective-permute-start | bytes 196616 | tf_op jit(solution)/shard_map/ppermute | solution.py:12
  31.6 151.8 %collective-permute-start.6 = (bf16[1,8,4096]{2,1,0:T(8,128)(2,1)}, bf16[1,8,4096]{2,1,0:T(8,128)(2,1)}, u32[]{:S(2)}, u32[]{:S(2)}) collective-permute-start(bf16[1,8,4096]{2,1,0:T(8,128)(2,1)} %slice.3382), channel_id=1, source_target_pairs={{0,4},{4,8},{8,12},{12,16},{16,20},{20,24},{24,28},{28,32},{32,36}... | collective-permute-start | bytes 196616 | tf_op jit(solution)/shard_map/ppermute | solution.py:12
  35.6 89.6 %collective-permute-start = (s32[8]{0:T(128)}, s32[8]{0:T(128)}, u32[]{:S(2)}, u32[]{:S(2)}) collective-permute-start(s32[8]{0:T(128)} %param.118), channel_id=1, source_target_pairs={{0,4},{4,0},{8,12},{12,8},{16,20},{20,16},{24,28},{28,24},{32,36},... | collective-permute-start | bytes 104 | tf_op jit(solution)/shard_map/ppermute | solution.py:27
  35.7 20.5 %copy-start.10 = (s32[8,27]{1,0:T(8,128)}, s32[8,27]{1,0:T(8,128)S(1)}, u32[]{:S(2)}) copy-start(s32[8,27]{1,0:T(8,128)S(1)} %get-tuple-element.761) | copy-start | bytes 2596
  35.7 20.5 %copy-start.12 = (s32[8,27]{1,0:T(8,128)}, s32[8,27]{1,0:T(8,128)S(1)}, u32[]{:S(2)}) copy-start(s32[8,27]{1,0:T(8,128)S(1)} %get-tuple-element.760) | copy-start | bytes 2596
  35.7 20.5 %copy-start.29 = (pred[8,27]{1,0:T(8,128)(4,1)}, pred[8,27]{1,0:T(8,128)(4,1)S(1)}, u32[]{:S(2)}) copy-start(pred[8,27]{1,0:T(8,128)(4,1)S(1)} %get-tuple-element.762) | copy-start | bytes 652
  89.0 15.6 %copy-start.47 = (bf16[8,64,8,1,8]{1,0,4,3,2:T(8,128)(2,1)S(1)}, bf16[8,64,8,1,8]{1,0,4,3,2:T(8,128)(2,1)}, u32[]{:S(2)}) copy-start(bf16[8,64,8,1,8]{1,0,4,3,2:T(8,128)(2,1)} %get-tuple-element.909) | copy-start | bytes 196612
  112.7 27.0 %copy-start.194 = (s32[8]{0:T(128)S(1)}, s32[8]{0:T(128)}, u32[]{:S(2)}) copy-start(s32[8]{0:T(128)} %get-tuple-element.693) | copy-start | bytes 100
  113.4 28.2 %copy-start.49 = (bf16[8,128,64]{1,2,0:T(8,128)(2,1)S(1)}, bf16[8,128,64]{1,2,0:T(8,128)(2,1)}, u32[]{:S(2)}) copy-start(bf16[8,128,64]{1,2,0:T(8,128)(2,1)} %param.120) | copy-start | bytes 393220
  114.2 217.3 %copy-start.25 = (f32[8,512]{0,1:T(8,128)}, f32[8,512]{0,1:T(8,128)S(1)}, u32[]{:S(2)}) copy-start(f32[8,512]{0,1:T(8,128)S(1)} %copy.274) | copy-start | bytes 49156
  125.2 66.9 %collective-permute-start.7 = (bf16[1,8,4096]{2,1,0:T(8,128)(2,1)}, bf16[1,8,4096]{2,1,0:T(8,128)(2,1)}, u32[]{:S(2)}, u32[]{:S(2)}) collective-permute-start(bf16[1,8,4096]{2,1,0:T(8,128)(2,1)} %slice.3430), channel_id=1, source_target_pairs={{1,0},{2,1},{3,2},{5,4},{6,5},{7,6},{9,8},{10,9},{11,10},{13,12},{... | collective-permute-start | bytes 196616 | tf_op jit(solution)/shard_map/ppermute | solution.py:15
  147.2 8.0 %collective-permute-start.3 = (bf16[4,1,8,512]{3,2,1,0:T(8,128)(2,1)S(1)}, bf16[4,1,8,512]{3,2,1,0:T(8,128)(2,1)S(1)}, u32[]{:S(2)}, u32[]{:S(2)}) collective-permute-start(bf16[4,1,8,512]{3,2,1,0:T(8,128)(2,1)S(1)} %get-tuple-element.919), channel_id=1, source_target_pairs={{0,1},{1,2},{2,3},{4,5},{5,6},{6,7},{8,9},{9,10},{10,11},{12,13},{... | collective-permute-start | bytes 98312 | tf_op jit(solution)/shard_map/ppermute | solution.py:12
  151.2 7.0 collective-permute-start.4
  155.3 50.8 %collective-permute-start.8 = (bf16[1,8,4096]{2,1,0:T(8,128)(2,1)S(1)}, bf16[1,8,4096]{2,1,0:T(8,128)(2,1)}, u32[]{:S(2)}, u32[]{:S(2)}) collective-permute-start(bf16[1,8,4096]{2,1,0:T(8,128)(2,1)S(1)} %slice.3505), channel_id=1, source_target_pairs={{4,0},{8,4},{12,8},{16,12},{20,16},{24,20},{28,24},{32,28},{36,32}... | collective-permute-start | bytes 196616 | tf_op jit(solution)/shard_map/ppermute | solution.py:15
  158.2 171.3 %collective-permute-start.10 = (bf16[8,64,512]{2,1,0:T(8,128)(2,1)}, bf16[8,64,512]{2,1,0:T(8,128)(2,1)}, u32[]{:S(2)}, u32[]{:S(2)}) collective-permute-start(bf16[8,64,512]{2,1,0:T(8,128)(2,1)} %copy.282), channel_id=1, source_target_pairs={{0,4},{4,0},{8,12},{12,8},{16,20},{20,16},{24,28},{28,24},{32,36},... | collective-permute-start | bytes 1572872 | tf_op jit(solution)/shard_map/ppermute | solution.py:27
  226.3 17.5 %copy-start.18 = (bf16[8,64,8,1]{3,2,1,0:T(8,128)(2,1)S(1)}, bf16[8,64,8,1]{3,2,1,0:T(8,128)(2,1)}, u32[]{:S(2)}) copy-start(bf16[8,64,8,1]{3,2,1,0:T(8,128)(2,1)} %get-tuple-element.901) | copy-start | bytes 24580
  273.4 15.8 %copy-start.94 = (pred[8]{0:T(512)(128)(4,1)S(1)}, pred[8]{0:T(512)(128)(4,1)}, u32[]{:S(2)}) copy-start(pred[8]{0:T(512)(128)(4,1)} %get-tuple-element.667) | copy-start | bytes 28
  273.4 17.5 %copy-start.92 = (pred[8]{0:T(512)(128)(4,1)S(1)}, pred[8]{0:T(512)(128)(4,1)}, u32[]{:S(2)}) copy-start(pred[8]{0:T(512)(128)(4,1)} %get-tuple-element.666) | copy-start | bytes 28
  274.1 19.8 %copy-start.9 = (bf16[8,64,512]{1,0,2:T(8,128)(2,1)S(1)}, bf16[8,64,512]{1,0,2:T(8,128)(2,1)}, u32[]{:S(2)}) copy-start(bf16[8,64,512]{1,0,2:T(8,128)(2,1)} %copy-done.8) | copy-start | bytes 1572868
  274.1 19.8 %copy-start.98 = (pred[8]{0:T(512)(128)(4,1)S(1)}, pred[8]{0:T(512)(128)(4,1)}, u32[]{:S(2)}) copy-start(pred[8]{0:T(512)(128)(4,1)} %get-tuple-element.963) | copy-start | bytes 28
  298.6 16.0 %copy-start.62 = (bf16[8,64]{1,0:T(8,128)(2,1)S(1)}, bf16[8,64]{1,0:T(8,128)(2,1)}, u32[]{:S(2)}) copy-start(bf16[8,64]{1,0:T(8,128)(2,1)} %gather_fusion.40) | copy-start | bytes 3076
  298.6 16.0 %copy-start.134 = (pred[8]{0:T(512)(128)(4,1)S(1)}, pred[8]{0:T(512)(128)(4,1)}, u32[]{:S(2)}) copy-start(pred[8]{0:T(512)(128)(4,1)} %get-tuple-element.683) | copy-start | bytes 28
  298.6 16.0 %copy-start.140 = (pred[8]{0:T(512)(128)(4,1)S(1)}, pred[8]{0:T(512)(128)(4,1)}, u32[]{:S(2)}) copy-start(pred[8]{0:T(512)(128)(4,1)} %get-tuple-element.713) | copy-start | bytes 28
  298.6 16.0 %copy-start.142 = (pred[8]{0:T(512)(128)(4,1)S(1)}, pred[8]{0:T(512)(128)(4,1)}, u32[]{:S(2)}) copy-start(pred[8]{0:T(512)(128)(4,1)} %get-tuple-element.722) | copy-start | bytes 28
  298.6 17.2 %copy-start.96 = (pred[8]{0:T(512)(128)(4,1)S(1)}, pred[8]{0:T(512)(128)(4,1)}, u32[]{:S(2)}) copy-start(pred[8]{0:T(512)(128)(4,1)} %get-tuple-element.678) | copy-start | bytes 28
  298.6 17.2 %copy-start.104 = (pred[8]{0:T(512)(128)(4,1)S(1)}, pred[8]{0:T(512)(128)(4,1)}, u32[]{:S(2)}) copy-start(pred[8]{0:T(512)(128)(4,1)} %get-tuple-element.711) | copy-start | bytes 28
  298.6 17.2 %copy-start.106 = (pred[8]{0:T(512)(128)(4,1)S(1)}, pred[8]{0:T(512)(128)(4,1)}, u32[]{:S(2)}) copy-start(pred[8]{0:T(512)(128)(4,1)} %get-tuple-element.724) | copy-start | bytes 28
  298.6 18.6 %copy-start.61 = (bf16[8,64]{1,0:T(8,128)(2,1)S(1)}, bf16[8,64]{1,0:T(8,128)(2,1)}, u32[]{:S(2)}) copy-start(bf16[8,64]{1,0:T(8,128)(2,1)} %gather_fusion.46) | copy-start | bytes 3076
  298.6 18.6 %copy-start.128 = (pred[8]{0:T(512)(128)(4,1)S(1)}, pred[8]{0:T(512)(128)(4,1)}, u32[]{:S(2)}) copy-start(pred[8]{0:T(512)(128)(4,1)} %get-tuple-element.957) | copy-start | bytes 28
  298.6 18.6 %copy-start.138 = (pred[8]{0:T(512)(128)(4,1)S(1)}, pred[8]{0:T(512)(128)(4,1)}, u32[]{:S(2)}) copy-start(pred[8]{0:T(512)(128)(4,1)} %get-tuple-element.672) | copy-start | bytes 28
  298.7 18.6 %copy-start.145 = (pred[8]{0:T(512)(128)(4,1)S(1)}, pred[8]{0:T(512)(128)(4,1)}, u32[]{:S(2)}) copy-start(pred[8]{0:T(512)(128)(4,1)} %get-tuple-element.684) | copy-start | bytes 28
  385.9 15.4 %copy-start.54 = (bf16[8,64,1,1,8]{1,0,4,3,2:T(8,128)(2,1)S(1)}, bf16[8,64,1,1,8]{1,0,4,3,2:T(8,128)(2,1)}, u32[]{:S(2)}) copy-start(bf16[8,64,1,1,8]{1,0,4,3,2:T(8,128)(2,1)} %get-tuple-element.873) | copy-start | bytes 24580
  385.9 19.3 %copy-start.53 = (bf16[8,64,1,1,8]{1,0,4,3,2:T(8,128)(2,1)S(1)}, bf16[8,64,1,1,8]{1,0,4,3,2:T(8,128)(2,1)}, u32[]{:S(2)}) copy-start(bf16[8,64,1,1,8]{1,0,4,3,2:T(8,128)(2,1)} %get-tuple-element.875) | copy-start | bytes 24580
  385.9 19.6 %copy-start.52 = (bf16[8,64,1,1,8]{1,0,4,3,2:T(8,128)(2,1)S(1)}, bf16[8,64,1,1,8]{1,0,4,3,2:T(8,128)(2,1)}, u32[]{:S(2)}) copy-start(bf16[8,64,1,1,8]{1,0,4,3,2:T(8,128)(2,1)} %get-tuple-element.874) | copy-start | bytes 24580
  385.9 21.9 %copy-start.4 = (bf16[8,64,512]{1,0,2:T(8,128)(2,1)S(1)}, bf16[8,64,512]{1,0,2:T(8,128)(2,1)}, u32[]{:S(2)}) copy-start(bf16[8,64,512]{1,0,2:T(8,128)(2,1)} %copy-done.3) | copy-start | bytes 1572868
  400.9 15.6 %copy-start.6 = (bf16[8,64,512]{1,0,2:T(8,128)(2,1)S(1)}, bf16[8,64,512]{1,0,2:T(8,128)(2,1)}, u32[]{:S(2)}) copy-start(bf16[8,64,512]{1,0,2:T(8,128)(2,1)} %get-tuple-element.818) | copy-start | bytes 1572868
  401.6 6.2 collective-permute-start.11
  405.9 5.1 collective-permute-start.12
  410.9 25.8 %collective-permute-start.13 = (bf16[4,1,8,512]{3,2,1,0:T(8,128)(2,1)S(1)}, bf16[4,1,8,512]{3,2,1,0:T(8,128)(2,1)S(1)}, u32[]{:S(2)}, u32[]{:S(2)}) collective-permute-start(bf16[4,1,8,512]{3,2,1,0:T(8,128)(2,1)S(1)} %get-tuple-element.917), channel_id=1, source_target_pairs={{0,1},{1,2},{2,3},{4,5},{5,6},{6,7},{8,9},{9,10},{10,11},{12,13},{... | collective-permute-start | bytes 98312 | tf_op jit(solution)/shard_map/ppermute | solution.py:12
  415.2 22.8 %collective-permute-start.14 = (bf16[4,1,8,512]{3,2,1,0:T(8,128)(2,1)S(1)}, bf16[4,1,8,512]{3,2,1,0:T(8,128)(2,1)S(1)}, u32[]{:S(2)}, u32[]{:S(2)}) collective-permute-start(bf16[4,1,8,512]{3,2,1,0:T(8,128)(2,1)S(1)} %get-tuple-element.918), channel_id=1, source_target_pairs={{1,0},{2,1},{3,2},{5,4},{6,5},{7,6},{9,8},{10,9},{11,10},{13,12},{... | collective-permute-start | bytes 98312 | tf_op jit(solution)/shard_map/ppermute | solution.py:15
  418.1 159.3 %collective-permute-start.9 = (bf16[8,64,512]{2,1,0:T(8,128)(2,1)}, bf16[8,64,512]{2,1,0:T(8,128)(2,1)}, u32[]{:S(2)}, u32[]{:S(2)}) collective-permute-start(bf16[8,64,512]{2,1,0:T(8,128)(2,1)} %copy.275), channel_id=1, source_target_pairs={{0,4},{4,0},{8,12},{12,8},{16,20},{20,16},{24,28},{28,24},{32,36},... | collective-permute-start | bytes 1572872 | tf_op jit(solution)/shard_map/ppermute | solution.py:27
  420.7 32.9 %collective-permute-start.15 = (bf16[1,8,4096]{2,1,0:T(8,128)(2,1)}, bf16[1,8,4096]{2,1,0:T(8,128)(2,1)}, u32[]{:S(2)}, u32[]{:S(2)}) collective-permute-start(bf16[1,8,4096]{2,1,0:T(8,128)(2,1)} %slice.3586), channel_id=1, source_target_pairs={{0,1},{1,2},{2,3},{4,5},{5,6},{6,7},{8,9},{9,10},{10,11},{12,13},{... | collective-permute-start | bytes 196616 | tf_op jit(solution)/shard_map/ppermute | solution.py:12
  428.0 30.9 %collective-permute-start.16 = (bf16[1,8,4096]{2,1,0:T(8,128)(2,1)}, bf16[1,8,4096]{2,1,0:T(8,128)(2,1)}, u32[]{:S(2)}, u32[]{:S(2)}) collective-permute-start(bf16[1,8,4096]{2,1,0:T(8,128)(2,1)} %slice.3589), channel_id=1, source_target_pairs={{0,4},{4,8},{8,12},{12,16},{16,20},{20,24},{24,28},{28,32},{32,36}... | collective-permute-start | bytes 196616 | tf_op jit(solution)/shard_map/ppermute | solution.py:12
  436.8 30.8 %collective-permute-start.17 = (bf16[1,8,4096]{2,1,0:T(8,128)(2,1)}, bf16[1,8,4096]{2,1,0:T(8,128)(2,1)}, u32[]{:S(2)}, u32[]{:S(2)}) collective-permute-start(bf16[1,8,4096]{2,1,0:T(8,128)(2,1)} %slice.3613), channel_id=1, source_target_pairs={{1,0},{2,1},{3,2},{5,4},{6,5},{7,6},{9,8},{10,9},{11,10},{13,12},{... | collective-permute-start | bytes 196616 | tf_op jit(solution)/shard_map/ppermute | solution.py:15
  438.1 42.9 %collective-permute-start.18 = (bf16[1,8,4096]{2,1,0:T(8,128)(2,1)S(1)}, bf16[1,8,4096]{2,1,0:T(8,128)(2,1)}, u32[]{:S(2)}, u32[]{:S(2)}) collective-permute-start(bf16[1,8,4096]{2,1,0:T(8,128)(2,1)S(1)} %slice.3651), channel_id=1, source_target_pairs={{4,0},{8,4},{12,8},{16,12},{20,16},{24,20},{28,24},{32,28},{36,32}... | collective-permute-start | bytes 196616 | tf_op jit(solution)/shard_map/ppermute | solution.py:15
  514.5 16.7 %copy-start.93 = (pred[8]{0:T(512)(128)(4,1)S(1)}, pred[8]{0:T(512)(128)(4,1)}, u32[]{:S(2)}) copy-start(pred[8]{0:T(512)(128)(4,1)} %get-tuple-element.666) | copy-start | bytes 28
  514.5 19.7 %copy-start.5 = (bf16[8,64,512]{1,0,2:T(8,128)(2,1)S(1)}, bf16[8,64,512]{1,0,2:T(8,128)(2,1)}, u32[]{:S(2)}) copy-start(bf16[8,64,512]{1,0,2:T(8,128)(2,1)} %copy-done.3) | copy-start | bytes 1572868
  514.5 19.7 %copy-start.99 = (pred[8]{0:T(512)(128)(4,1)S(1)}, pred[8]{0:T(512)(128)(4,1)}, u32[]{:S(2)}) copy-start(pred[8]{0:T(512)(128)(4,1)} %get-tuple-element.963) | copy-start | bytes 28
  550.4 16.4 %copy-start.83 = (pred[8]{0:T(512)(128)(4,1)S(1)}, pred[8]{0:T(512)(128)(4,1)}, u32[]{:S(2)}) copy-start(pred[8]{0:T(512)(128)(4,1)} %get-tuple-element.662) | copy-start | bytes 28
  550.4 17.2 %copy-start.81 = (pred[8]{0:T(512)(128)(4,1)S(1)}, pred[8]{0:T(512)(128)(4,1)}, u32[]{:S(2)}) copy-start(pred[8]{0:T(512)(128)(4,1)} %get-tuple-element.661) | copy-start | bytes 28
  551.1 17.5 %copy-start.79 = (pred[8]{0:T(512)(128)(4,1)S(1)}, pred[8]{0:T(512)(128)(4,1)}, u32[]{:S(2)}) copy-start(pred[8]{0:T(512)(128)(4,1)} %get-tuple-element.660) | copy-start | bytes 28
  551.1 18.3 %copy-start.135 = (pred[8]{0:T(512)(128)(4,1)S(1)}, pred[8]{0:T(512)(128)(4,1)}, u32[]{:S(2)}) copy-start(pred[8]{0:T(512)(128)(4,1)} %get-tuple-element.683) | copy-start | bytes 28
  551.1 18.3 %copy-start.141 = (pred[8]{0:T(512)(128)(4,1)S(1)}, pred[8]{0:T(512)(128)(4,1)}, u32[]{:S(2)}) copy-start(pred[8]{0:T(512)(128)(4,1)} %get-tuple-element.713) | copy-start | bytes 28
  551.1 18.3 %copy-start.143 = (pred[8]{0:T(512)(128)(4,1)S(1)}, pred[8]{0:T(512)(128)(4,1)}, u32[]{:S(2)}) copy-start(pred[8]{0:T(512)(128)(4,1)} %get-tuple-element.722) | copy-start | bytes 28
  551.1 19.0 %copy-start.97 = (pred[8]{0:T(512)(128)(4,1)S(1)}, pred[8]{0:T(512)(128)(4,1)}, u32[]{:S(2)}) copy-start(pred[8]{0:T(512)(128)(4,1)} %get-tuple-element.678) | copy-start | bytes 28
  551.1 19.0 %copy-start.105 = (pred[8]{0:T(512)(128)(4,1)S(1)}, pred[8]{0:T(512)(128)(4,1)}, u32[]{:S(2)}) copy-start(pred[8]{0:T(512)(128)(4,1)} %get-tuple-element.711) | copy-start | bytes 28
  551.2 19.0 %copy-start.107 = (pred[8]{0:T(512)(128)(4,1)S(1)}, pred[8]{0:T(512)(128)(4,1)}, u32[]{:S(2)}) copy-start(pred[8]{0:T(512)(128)(4,1)} %get-tuple-element.724) | copy-start | bytes 28
  551.2 19.8 %copy-start.129 = (pred[8]{0:T(512)(128)(4,1)S(1)}, pred[8]{0:T(512)(128)(4,1)}, u32[]{:S(2)}) copy-start(pred[8]{0:T(512)(128)(4,1)} %get-tuple-element.957) | copy-start | bytes 28
  551.2 19.8 %copy-start.139 = (pred[8]{0:T(512)(128)(4,1)S(1)}, pred[8]{0:T(512)(128)(4,1)}, u32[]{:S(2)}) copy-start(pred[8]{0:T(512)(128)(4,1)} %get-tuple-element.672) | copy-start | bytes 28
  (168 other events, 1415.0 us)
Sparse Core Ops, SparseCore 0:
  582.6 153.2 all-reduce.4
where the time goes:
time: 758 us; the launch traced here: 747 us
  local copies, waits for them, and re-layouts  344 us (45%)
  other arithmetic  155 us (20%)
  waiting for transfers between devices  147 us (19%)
  starting transfers between devices  59.5 us (8%)
  matrix products  24.7 us (3%)
  between operations  17.5 us (2%)
    psum x1, waiting for transfers between devices, shards(): w_sub_sum, w_down_sum = lax.psum((w_sub_part, w_down_part), ('gz', 'gy'))  143 us
    unnamed x503, local copies, waits for them, and re-layouts  68.1 us
    scatter x48, other arithmetic, build_padded(): padded = padded.at[:, :, into_z, into_y, into_x].set(portion)  61.1 us
    select_n x2, other arithmetic, build_padded(): jnp.where(local_flag[:, :, None, None, None, None], nearby, jnp.zeros_lik...  51.8 us
    squeeze x4, local copies, waits for them, and re-layouts, build_padded(): portion = nearby[:, column][:, :, from_z, from_y, from_x]  43.7 us
    ppermute x8, starting transfers between devices, padded_2(): lax.ppermute(lax.slice_in_dim(block, block.shape[dim] - width, None, axis...  33 us
    gather x36, local copies, waits for them, and re-layouts, build_padded(): remote = z_faces[side_z][:, :, from_y, from_x][chosen][:, :, None]  29.3 us
    gather x36, local copies, waits for them, and re-layouts, build_padded(): remote = y_faces[side_y][:, :, from_z, from_x][chosen][:, :, :, None]  28.7 us
  transfers between devices with their start and end apart: 20, of which 2 were waited for; matrix products, arithmetic and copies ran while one was open for 58% of the time, Pallas kernels for 0%

commit v1 on v0

v1 whole, which is shorter than its diff:
```python
import functools

import jax
import jax.numpy as jnp
import numpy as np
from jax import lax
from jax.experimental import pallas as pl
from jax.experimental.pallas import tpu as pltpu
from jax.sharding import PartitionSpec as P

MESH = pl.DeviceIdType.MESH
BF = jnp.bfloat16
F32 = jnp.float32

Y_LOW, Y_HIGH, ZERO, Z_LOW, Z_HIGH, DIAGONAL, BANK = 64, 128, 192, 200, 208, 216, 248


def one_hot(shape, pairs):
    out = np.zeros(shape, np.float32)
    for row, column in pairs:
        out[row, column] = 1.0
    return jnp.asarray(out, BF)


def lane(y, x):
    return 10 * (y + 1) + x + 1


def permutations():
    wrap = [
        (64 * h + 8 * ((yp - 1) % 8) + (xp - 1) % 8, 128 * h + 10 * yp + xp)
        for h in range(2) for yp in range(10) for xp in range(10)
    ]
    rewrap = [
        (lane((yp - 1) % 8, (xp - 1) % 8), 10 * yp + xp) for yp in range(10) for xp in range(10)
    ]
    native = [
        (128 * h + lane(y, x), 64 * h + 8 * y + x)
        for h in range(2) for y in range(8) for x in range(8)
    ]
    pack = [
        (128 * z + 10 * (0 if side == 0 else 9) + xp, 128 * side + 10 * z + xp)
        for side in range(2) for z in range(8) for xp in range(10)
    ]
    unpack = [
        [(10 * z + xp, 128 * z + 90 * side + xp) for z in range(8) for xp in range(10)]
        for side in range(2)
    ]
    phase, octant = [], []
    for z in range(8):
        for y in range(8):
            for x in range(8):
                k = 4 * (z % 2) + 2 * (y % 2) + x % 2
                v = 16 * (z // 2) + 4 * (y // 2) + x // 2
                phase.append((128 * z + lane(y, x), 64 * k + v))
                k = 4 * (z // 4) + 2 * (y // 4) + x // 4
                v = 16 * (z % 4) + 4 * (y % 4) + x % 4
                octant.append((64 * k + v, 64 * z + 8 * y + x))
    flip = lambda pairs: [(b, a) for a, b in pairs]
    return (
        one_hot((128, 256), wrap),
        one_hot((128, 128), rewrap),
        one_hot((256, 128), native),
        one_hot((1024, 256), pack),
        one_hot((128, 1024), unpack[0]),
        one_hot((128, 1024), unpack[1]),
        one_hot((1024, 512), phase),
        one_hot((512, 1024), flip(phase)),
        one_hot((512, 512), octant),
        one_hot((512, 512), flip(octant)),
    )


def dot(a, b):
    return jnp.dot(a, b, preferred_element_type=F32)


def dot_nt(a, b):
    return lax.dot_general(a, b, (((1,), (1,)), ((), ())), preferred_element_type=F32)


def roll(x, shift):
    return pltpu.roll(x, shift % 128, x.ndim - 1)


def body(
    scale,
    feat, occ, nbr, dest_v, dest_s, w_sub, w_down, cgrad,
    p_wrap, p_rewrap, p_native, p_pack, p_un0, p_un1, p_phase, p_unphase, p_oct, p_unoct,
    coarse, feat_grad, ws_out, wd_out,
    bank1, bank2, ysend, ydst, zsend, dsend, drecv, idx_v, idx_s, inv_v, inv_s, dest_buf, dest_in,
    cg_bank, og_in, og_all, og, ag_ph, ag, occ_p, r_buf, act, phases, pg, wf, wb, wd, wdt,
    bl, bl_in, bl_bank, fg, wg, ws_src, ws_ra, ws_red, ws_rb, ws_gb, ws_ga,
    wd_src, wd_ra, wd_red, wd_rb, wd_gb, wd_ga,
    h_send, h_recv, c_send, c_recv, idx_sem, r_send, r_recv,
):
    gz, gy = lax.axis_index("gz"), lax.axis_index("gy")
    cy, cz, core = gz // 8, (gz // 2) % 4, gz % 2
    nz, ny = 32, 4

    def at(dz, dy):
        return {"gz": (gz + dz + nz) % nz, "gy": (gy + dy + ny) % ny}

    partner = {"gz": gz + 1 - 2 * core, "gy": gy}
    halo_steps = [(dz, dy) for dz in (-1, 0, 1) for dy in (-1, 0, 1) if (dz, dy) != (0, 0)]
    a_steps = [(dc, dx) for dx in range(4) for dc in range(2) if (dc, dx) != (0, 0)]
    b_steps = [(dy, dz) for dy in range(4) for dz in range(4) if (dy, dz) != (0, 0)]

    def a_peer(dc, dx):
        return {"gz": gz - core + (core + dc) % 2, "gy": (gy + dx) % 4}

    def b_peer(dy, dz):
        return {"gz": ((cy + dy) % 4 * 4 + (cz + dz) % 4) * 2 + core, "gy": gy}

    barrier = pltpu.get_barrier_semaphore()
    for device in (
        [at(*s) for s in halo_steps] + [a_peer(*s) for s in a_steps] + [b_peer(*s) for s in b_steps]
    ):
        pl.semaphore_signal(barrier, inc=1, device_id=device, device_id_type=MESH)

    def send(src, dst, send_sem, recv_sem, device):
        copy = pltpu.make_async_remote_copy(
            src_ref=src, dst_ref=dst, send_sem=send_sem, recv_sem=recv_sem,
            device_id=device, device_id_type=MESH,
        )
        copy.start()
        return copy

    lanes = lax.broadcasted_iota(jnp.int32, (64, 128), 1)
    low_half = lax.broadcasted_iota(jnp.int32, (128, 128), 1) < 64
    xp = lanes - 10 * lax.shift_right_logical(lanes * 205, 11)
    first, last = xp == 0, xp == 9
    yp_low, yp_high = lanes < 10, lanes >= 90
    center_row = lax.broadcasted_iota(jnp.int32, (8, 128), 1)
    center_x = center_row - 10 * lax.shift_right_logical(center_row * 205, 11)
    center = (center_row > 10) & (center_row < 89) & (center_x > 0) & (center_x < 9)

    table = nbr[...]
    owner = table // 8
    slot = table - owner * 8
    step_z = owner // 4 - gz
    step_y = owner - owner // 4 * 4 - gy
    column = lax.broadcasted_iota(jnp.int32, (8, 27), 1)
    part_a = column // 9
    edge_z = jnp.where(part_a == 0, 7, 0)
    on_z = Z_LOW + jnp.where(step_z > 0, 8, 0) + slot
    on_diagonal = DIAGONAL + jnp.where(step_z > 0, 16, 0) + jnp.where(step_y > 0, 8, 0) + slot
    same_z = jnp.where(step_y == 0, 0, jnp.where(step_y < 0, Y_LOW, Y_HIGH)) + slot * 8 + edge_z
    index = jnp.where(step_z == 0, same_z, jnp.where(step_y == 0, on_z, on_diagonal))
    index = jnp.where((table < 0) | ((part_a == 1) & (index > ZERO)), ZERO, index)
    idx_v[...] = jnp.zeros_like(idx_v)
    idx_v[:, 0:27] = index
    idx_copy = pltpu.make_async_copy(idx_v, idx_s, idx_sem.at[0])
    idx_copy.start()

    for q in range(4):
        part = feat[:, :, 128 * q:128 * q + 128]
        flag = occ[:, 128 * q:128 * q + 128].astype(F32).astype(BF)
        rows = [part[t] * flag[t:t + 1] for t in range(8)]
        planes = dot(jnp.concatenate(rows, axis=0), p_wrap[...]).astype(BF)
        flags = dot(flag, p_wrap[...])
        for h in range(2):
            flag_plane = jnp.where(center, flags[:, 128 * h:128 * h + 128], 0.0)
            for t in range(8):
                occ_p[t, :, 128 * (2 * q + h):128 * (2 * q + h) + 128] = flag_plane[t:t + 1]
                bank1[8 * t + 2 * q + h] = planes[64 * t:64 * t + 64, 128 * h:128 * h + 128]

    dest_buf[0] = jnp.zeros((8, 128), jnp.int32) - 1
    dest_buf[0, 0:1, 0:8] = dest_v[...]
    for bank in (bank1, bank2):
        bank[ZERO:ZERO + 8] = jnp.zeros((8, 64, 128), BF)

    pl.semaphore_wait(barrier, len(halo_steps) + len(a_steps) + len(b_steps))

    dest_send = send(dest_buf.at[0], dest_buf.at[1], c_send.at[0], c_recv.at[0], partner)
    cg_send = send(cgrad, cg_bank.at[pl.ds(8, 8)], c_send.at[1], c_recv.at[1], partner)
    local_cg = pltpu.make_async_copy(cgrad, cg_bank.at[pl.ds(0, 8)], idx_sem.at[1])
    local_cg.start()

    def publish(bank, which):
        copies = []
        total = None
        for q in range(4):
            both = jnp.concatenate(
                [
                    jnp.concatenate([bank[8 * t + 2 * q], bank[8 * t + 2 * q + 1]], axis=1)
                    for t in range(8)
                ],
                axis=0,
            )
            term = dot(both, p_pack[256 * q:256 * q + 256, :])
            total = term if total is None else total + term
        rows = total.astype(BF)
        for side in range(2):
            for t in range(8):
                ysend[which, side, t] = rows[64 * t:64 * t + 64, 128 * side:128 * side + 128]
                zsend[which, side, t] = bank[8 * t + (7 if side == 0 else 0)]
        for side in range(2):
            up = 1 - 2 * side
            copies.append(
                send(
                    ysend.at[which, side], ydst.at[which, side],
                    h_send.at[which, side], h_recv.at[which, side], at(0, up),
                )
            )
            copies.append(
                send(
                    zsend.at[which, side], bank.at[pl.ds(Z_LOW if side == 0 else Z_HIGH, 8)],
                    h_send.at[which, 2 + side], h_recv.at[which, 2 + side], at(up, 0),
                )
            )
        for side_z in range(2):
            for side_y in range(2):
                number = 2 * side_z + side_y
                gathered = None
                for t in range(8):
                    piece = total[64 * t:64 * t + 64, 128 * side_y:128 * side_y + 128]
                    piece = roll(piece, 16 * t - (70 if side_z == 0 else 0))
                    piece = jnp.where((lanes >= 16 * t) & (lanes < 16 * t + 10), piece, 0.0)
                    gathered = piece if gathered is None else gathered + piece
                dsend[which, number] = gathered.astype(BF)
                copies.append(
                    send(
                        dsend.at[which, number], drecv.at[which, number],
                        h_send.at[which, 4 + number], h_recv.at[which, 4 + number],
                        at(1 - 2 * side_z, 1 - 2 * side_y),
                    )
                )
        return copies

    def receive(bank, which, copies):
        for copy in copies:
            copy.wait_recv()
        for side in range(2):
            rows = ydst[which, side].reshape(512, 128)
            for q in range(4):
                planes = dot(rows, (p_un0, p_un1)[side][:, 256 * q:256 * q + 256]).astype(BF)
                for t in range(8):
                    for h in range(2):
                        bank[(Y_LOW, Y_HIGH)[side] + 8 * t + 2 * q + h] = planes[
                            64 * t:64 * t + 64, 128 * h:128 * h + 128
                        ]
        for side_z in range(2):
            for side_y in range(2):
                number = 2 * side_z + side_y
                packed = drecv[which, number].astype(F32)
                for t in range(8):
                    bank[DIAGONAL + 8 * number + t] = roll(packed, 90 * side_y - 16 * t).astype(BF)

    def assemble(bank, t):
        masks = {0: (yp_low,), 1: (), 2: (yp_high,)}
        for zp in range(10):
            a = 0 if zp == 0 else (2 if zp == 9 else 1)
            rows = []
            for b in range(3):
                loaded = []
                for c in range(3):
                    place = idx_s[t, 9 * a + 3 * b + c] + (zp - 1 if a == 1 else 0)
                    loaded.append(bank[place])
                rows.append(jnp.where(first, loaded[0], jnp.where(last, loaded[2], loaded[1])))
            plane = jnp.where(yp_low, rows[0], jnp.where(yp_high, rows[2], rows[1]))
            wide = plane.astype(F32)
            columns = slice(128 * zp, 128 * zp + 128)
            r_buf[t, 0:64, columns] = roll(wide, 10).astype(BF)
            r_buf[t, 64:128, columns] = plane
            r_buf[t, 128:192, columns] = roll(wide, -10).astype(BF)

    def convolve(weights, t, q):
        total = None
        for a in range(3):
            term = dot(weights[a], r_buf[t, :, 128 * a + 256 * q:128 * a + 256 * q + 256])
            total = term if total is None else total + term
        parts = []
        for h in range(2):
            y = total[:, 128 * h:128 * h + 128]
            parts.append(roll(y[0:64], 1) + y[64:128] + roll(y[128:192], -1))
        return parts

    halo = publish(bank1, 0)

    for a in range(3):
        for c in range(3):
            wf[a, 64 * c:64 * c + 64, :] = jnp.concatenate(
                [w_sub[9 * a + 3 * b + c].astype(F32) for b in range(3)], axis=1
            ).astype(BF)
        turned = jnp.concatenate(
            [
                jnp.concatenate(
                    [w_sub[9 * (2 - a) + 3 * (2 - b) + 2 - c].astype(F32) for c in range(3)], axis=1
                )
                for b in range(3)
            ],
            axis=0,
        )
        wb[a] = turned.T.astype(BF)
    wide = jnp.concatenate([w_down[k].astype(F32) for k in range(8)], axis=1)
    wd[...] = wide.astype(BF)
    wdt[...] = wide.T.astype(BF)

    cg_bank[16] = jnp.zeros((128, 512), BF)
    idx_copy.wait()
    local_cg.wait()
    cg_send.wait_recv()
    base = gz * 4 + gy
    partner_index = (gz + 1 - 2 * core) * 4 + gy
    for t in range(8):
        d = dest_s[0, t]
        own = d // 8 - base * 8
        other = d // 8 - partner_index * 8
        chosen = jnp.where((other >= 0) & (other < 8), 8 + other, 16)
        chosen = jnp.where((own >= 0) & (own < 8), own, chosen)
        og_in[128 * t:128 * t + 128, :] = cg_bank[chosen]
    for q in range(2):
        split = dot(og_in[...], p_unoct[:, 256 * q:256 * q + 256]).astype(BF)
        for t in range(8):
            for h in range(2):
                og_all[4 * t + 2 * q + h] = split[128 * t:128 * t + 128, 128 * h:128 * h + 128]
    for j in range(4):
        halves = []
        for h in range(2):
            t = 2 * j + h
            d = dest_s[0, t]
            octant = d - d // 8 * 8
            piece = og_all[4 * t + octant // 2].astype(F32)
            odd = octant - octant // 2 * 2
            halves.append(jnp.where(odd == h, piece, roll(piece, 64)))
        og[:, 128 * j:128 * j + 128] = jnp.where(low_half, halves[0], halves[1]).astype(BF)
    low64 = lanes < 64
    for r in range(4):
        rows = dot(wdt[128 * r:128 * r + 128, :], og[...]).astype(BF).astype(F32)
        for j in range(4):
            even = rows[0:64, 128 * j:128 * j + 128]
            odd = rows[64:128, 128 * j:128 * j + 128]
            columns = slice(128 * r, 128 * r + 128)
            ag_ph[128 * j:128 * j + 64, columns] = jnp.where(low64, even, roll(odd, 64)).astype(BF)
            ag_ph[128 * j + 64:128 * j + 128, columns] = jnp.where(
                low64, roll(even, 64), odd
            ).astype(BF)
    for q in range(4):
        spread = dot(ag_ph[...], p_unphase[:, 256 * q:256 * q + 256]).astype(BF)
        for t in range(8):
            ag[t, :, 256 * q:256 * q + 256] = spread[64 * t:64 * t + 64]

    dest_send.wait_recv()
    dest_copy = pltpu.make_async_copy(dest_buf.at[1], dest_in, idx_sem.at[2])
    dest_copy.start()
    dest_copy.wait()
    place = lax.broadcasted_iota(jnp.int32, (8, 128), 1) + base * 64
    inverse = jnp.zeros((8, 128), jnp.int32) + 16
    for s in range(8):
        inverse = jnp.where(place == dest_s[0, s], s, inverse)
        inverse = jnp.where(place == dest_in[0, s], 8 + s, inverse)
    inv_v[...] = inverse
    inv_copy = pltpu.make_async_copy(inv_v, inv_s, idx_sem.at[3])
    inv_copy.start()

    receive(bank1, 0, halo)

    @pl.loop(0, 8)
    def _(t):
        assemble(bank1, t)
        for q in range(4):
            parts = convolve(wf, t, q)
            for h in range(2):
                z = 2 * q + h
                v = parts[h]
                on = occ_p[t, :, 128 * z:128 * z + 128]
                s = 1.0 / (1.0 + jnp.exp(-v))
                act[t, :, 128 * z:128 * z + 128] = jnp.where(on > 0.5, v * s, 0.0).astype(BF)
                g = ag[t, :, 128 * z:128 * z + 128].astype(F32)
                g = g * s * (1.0 + v * (1.0 - s))
                pg[8 * t + z] = jnp.where(on > 0.5, g, 0.0).astype(BF)

    @pl.loop(0, 8)
    def _(t):
        rows = pg[pl.ds(8 * t, 8)].reshape(512, 128)
        bank2[pl.ds(8 * t, 8)] = dot(rows, p_rewrap[...]).astype(BF).reshape(8, 64, 128)

    halo2 = publish(bank2, 1)

    for q in range(2):
        split = dot(act[...].reshape(512, 1024), p_phase[:, 256 * q:256 * q + 256])
        for j in range(4):
            for h in range(2):
                even = split[128 * j:128 * j + 64, 128 * h:128 * h + 128]
                odd = split[128 * j + 64:128 * j + 128, 128 * h:128 * h + 128]
                k = 4 * q + 2 * h
                columns = slice(128 * j, 128 * j + 128)
                phases[64 * k:64 * k + 64, columns] = jnp.where(
                    low64, even, roll(odd, 64)
                ).astype(BF)
                phases[64 * k + 64:64 * k + 128, columns] = jnp.where(
                    low64, roll(even, 64), odd
                ).astype(BF)
    bl[...] = dot(wd[...], phases[...]).astype(BF)
    bl_send = send(bl, bl_in, c_send.at[2], c_recv.at[2], partner)
    down = dot_nt(og[...], phases[...])
    for k in range(8):
        half = down[:, 128 * (k // 2):128 * (k // 2) + 128]
        half = half if k % 2 == 0 else roll(half, 64)
        wd_src[128 * k:128 * k + 128, :] = jnp.where(low_half, half, 0.0)

    def reducer(which, src, ra, red, rb, gb, ga):
        me_a, me_b = gy * 2 + core, cy * 4 + cz
        rows_a = pl.ds(pl.multiple_of(me_a * 128, 128), 128)
        rows_b = pl.ds(pl.multiple_of(me_b * 8, 8), 8)
        sems = lambda n: (r_send.at[which, n], r_recv.at[which, n])

        def start_a():
            copies = []
            for n, (dc, dx) in enumerate(a_steps):
                m = (gy + dx) % 4 * 2 + (core + dc) % 2
                rows = src.at[pl.ds(pl.multiple_of(m * 128, 128), 128)]
                copies.append(send(rows, ra.at[n], *sems(n), a_peer(dc, dx)))
            return copies

        def finish_a(copies):
            for copy in copies:
                copy.wait_recv()
            total = src[rows_a]
            for n in range(7):
                total = total + ra[n]
            red[...] = total

        def start_b():
            copies = []
            for n, (dy, dz) in enumerate(b_steps):
                j = (cy + dy) % 4 * 4 + (cz + dz) % 4
                rows = red.at[pl.ds(pl.multiple_of(j * 8, 8), 8)]
                copies.append(send(rows, rb.at[n], *sems(7 + n), b_peer(dy, dz)))
            return copies

        def finish_b(copies):
            for copy in copies:
                copy.wait_recv()
            total = red[rows_b]
            for n in range(15):
                total = total + rb[n]
            gb[rows_b] = total * scale

        def start_gb():
            return [
                send(gb.at[rows_b], gb.at[rows_b], *sems(22 + n), b_peer(dy, dz))
                for n, (dy, dz) in enumerate(b_steps)
            ]

        def finish_gb(copies):
            for copy in copies:
                copy.wait_recv()
            ga[rows_a] = gb[...]

        def start_ga():
            return [
                send(gb, ga.at[rows_a], *sems(37 + n), a_peer(dc, dx))
                for n, (dc, dx) in enumerate(a_steps)
            ]

        def finish_ga(copies):
            for copy in copies:
                copy.wait_recv()

        started = []
        starts, finishes = (start_a, start_b, start_gb, start_ga), (
            finish_a, finish_b, finish_gb, finish_ga
        )

        def step():
            n = len(started)
            if n > 0:
                finishes[n - 1](started[n - 1])
            if n < 4:
                started.append(starts[n]())

        def drain():
            for copies in started:
                for copy in copies:
                    copy.wait_send()

        return step, drain

    down_step, down_drain = reducer(1, wd_src, wd_ra, wd_red, wd_rb, wd_gb, wd_ga)
    sub_step, sub_drain = reducer(0, ws_src, ws_ra, ws_red, ws_rb, ws_gb, ws_ga)
    down_step()

    wg[...] = jnp.zeros_like(wg)

    @pl.loop(0, 8)
    def _(t):
        planes = [pg[8 * t + z].astype(F32) for z in range(8)]
        shifted = jnp.concatenate(
            [
                jnp.concatenate([roll(p, c - 1).astype(BF) for p in planes], axis=1)
                for c in range(3)
            ],
            axis=0,
        )
        for a in range(3):
            wg[a] += dot_nt(shifted, r_buf[t, :, 128 * a:128 * a + 1024])

    for a in range(3):
        ws_src[192 * a:192 * a + 192, :] = wg[a, :, 0:128]
    ws_src[576:768, :] = jnp.concatenate([wg[0, :, 128:192], wg[1, :, 128:192]], axis=1)
    ws_src[768:960, 0:64] = wg[2, :, 128:192]
    ws_src[768:960, 64:128] = jnp.zeros((192, 64), F32)
    ws_src[960:1024, :] = jnp.zeros((64, 128), F32)
    sub_step()

    receive(bank2, 1, halo2)
    down_step()

    def backward(low, high):
        @pl.loop(low, high)
        def _(t):
            assemble(bank2, t)
            for q in range(4):
                parts = convolve(wb, t, q)
                for h in range(2):
                    z = 2 * q + h
                    on = occ_p[t, :, 128 * z:128 * z + 128]
                    fg[t, :, 128 * z:128 * z + 128] = jnp.where(on > 0.5, parts[h], 0.0).astype(BF)

    backward(0, 3)
    sub_step()
    down_step()
    backward(3, 6)
    sub_step()
    down_step()
    backward(6, 8)
    for q in range(4):
        rows = dot(fg[:, :, 256 * q:256 * q + 256].reshape(512, 256), p_native[...])
        feat_grad[:, :, 128 * q:128 * q + 128] = rows.astype(BF).reshape(8, 64, 128)
    sub_step()
    down_step()

    inv_copy.wait()
    bl_send.wait_recv()
    bl_bank[16] = jnp.zeros((128, 128), BF)
    for source in range(2):
        blocks = (bl, bl_in)[source]
        for j in range(4):
            pair = blocks[:, 128 * j:128 * j + 128].astype(F32)
            turned = roll(pair, 64)
            bl_bank[8 * source + 2 * j] = jnp.where(low_half, pair, turned).astype(BF)
            bl_bank[8 * source + 2 * j + 1] = jnp.where(low_half, turned, pair).astype(BF)
    for c in range(8):
        for q in range(4):
            even = bl_bank[inv_s[0, 8 * c + 2 * q]]
            odd = bl_bank[inv_s[0, 8 * c + 2 * q + 1]]
            og_in[128 * c:128 * c + 128, 128 * q:128 * q + 128] = jnp.where(low_half, even, odd)
    for q in range(2):
        rows = dot(og_in[...], p_oct[:, 256 * q:256 * q + 256]).astype(BF)
        coarse[:, :, 256 * q:256 * q + 256] = rows.reshape(8, 128, 256)

    sub_step()
    for a in range(3):
        for c in range(3):
            for b in range(2):
                rows = slice(192 * a + 64 * c, 192 * a + 64 * c + 64)
                ws_out[9 * a + 3 * b + c] = ws_ga[rows, 64 * b:64 * b + 64]
            row, column = ((576, 0), (576, 64), (768, 0))[a]
            rows = slice(row + 64 * c, row + 64 * c + 64)
            ws_out[9 * a + 6 + c] = ws_ga[rows, column:column + 64]
    for k in range(8):
        wd_out[k] = wd_ga[128 * k:128 * k + 128, 0:64]
    for copy in halo + halo2 + [dest_send, cg_send, bl_send]:
        copy.wait_send()
    sub_drain()
    down_drain()


def shards(features, occupancy, neighbors, coarse_dest, w_sub, w_down, coarse_grad):
    devices = lax.axis_size("gz") * lax.axis_size("gy")
    scale = (features.shape[0] * devices * 512.0) ** -0.5
    dest = coarse_dest.reshape(1, 8)
    vmem, anywhere = pl.BlockSpec(memory_space=pltpu.VMEM), pl.BlockSpec(memory_space=pl.ANY)
    in_specs = [vmem, vmem, vmem, vmem, pl.BlockSpec(memory_space=pltpu.SMEM), vmem, vmem, anywhere]
    in_specs += [vmem] * 10
    reducing = [
        pltpu.VMEM((1024, 128), F32),
        pltpu.VMEM((7, 128, 128), F32),
        pltpu.VMEM((128, 128), F32),
        pltpu.VMEM((15, 8, 128), F32),
        pltpu.VMEM((128, 128), F32),
        pltpu.VMEM((1024, 128), F32),
    ]
    return pl.pallas_call(
        functools.partial(body, scale),
        out_shape=(
            jax.ShapeDtypeStruct((8, 128, 512), BF),
            jax.ShapeDtypeStruct((8, 64, 512), BF),
            jax.ShapeDtypeStruct((27, 64, 64), F32),
            jax.ShapeDtypeStruct((8, 128, 64), F32),
        ),
        in_specs=in_specs,
        out_specs=(vmem,) * 4,
        scratch_shapes=[
            pltpu.VMEM((BANK, 64, 128), BF),
            pltpu.VMEM((BANK, 64, 128), BF),
            pltpu.VMEM((2, 2, 8, 64, 128), BF),
            pltpu.VMEM((2, 2, 8, 64, 128), BF),
            pltpu.VMEM((2, 2, 8, 64, 128), BF),
            pltpu.VMEM((2, 4, 64, 128), BF),
            pltpu.VMEM((2, 4, 64, 128), BF),
            pltpu.VMEM((8, 128), jnp.int32),
            pltpu.SMEM((8, 128), jnp.int32),
            pltpu.VMEM((8, 128), jnp.int32),
            pltpu.SMEM((8, 128), jnp.int32),
            pltpu.VMEM((2, 8, 128), jnp.int32),
            pltpu.SMEM((8, 128), jnp.int32),
            pltpu.VMEM((17, 128, 512), BF),
            pltpu.VMEM((1024, 512), BF),
            pltpu.VMEM((32, 128, 128), BF),
            pltpu.VMEM((128, 512), BF),
            pltpu.VMEM((512, 512), BF),
            pltpu.VMEM((8, 64, 1024), BF),
            pltpu.VMEM((8, 1, 1024), F32),
            pltpu.VMEM((8, 192, 1280), BF),
            pltpu.VMEM((8, 64, 1024), BF),
            pltpu.VMEM((512, 512), BF),
            pltpu.VMEM((64, 64, 128), BF),
            pltpu.VMEM((3, 192, 192), BF),
            pltpu.VMEM((3, 192, 192), BF),
            pltpu.VMEM((128, 512), BF),
            pltpu.VMEM((512, 128), BF),
            pltpu.VMEM((128, 512), BF),
            pltpu.VMEM((128, 512), BF),
            pltpu.VMEM((17, 128, 128), BF),
            pltpu.VMEM((8, 64, 1024), BF),
            pltpu.VMEM((3, 192, 192), F32),
        ] + reducing + reducing + [
            pltpu.SemaphoreType.DMA((2, 8)),
            pltpu.SemaphoreType.DMA((2, 8)),
            pltpu.SemaphoreType.DMA((3,)),
            pltpu.SemaphoreType.DMA((3,)),
            pltpu.SemaphoreType.DMA((4,)),
            pltpu.SemaphoreType.DMA((2, 44)),
            pltpu.SemaphoreType.DMA((2, 44)),
        ],
        compiler_params=pltpu.CompilerParams(
            collective_id=0, has_side_effects=True, vmem_limit_bytes=60 * 1024 * 1024
        ),
        cost_estimate=pl.CostEstimate(flops=6 * 10**9, bytes_accessed=12 * 10**6, transcendentals=10**6),
        name="sparse_conv",
    )(features, occupancy, neighbors, dest, dest, w_sub, w_down, coarse_grad, *permutations())


def solution(mesh):
    return jax.shard_map(
        shards,
        mesh=mesh,
        in_specs=(
            P(("gz", "gy"), None, None),
            P(("gz", "gy"), None),
            P(("gz", "gy"), None),
            P(("gz", "gy")),
            P(),
            P(),
            P(("gz", "gy"), None, None),
        ),
        out_specs=(P(("gz", "gy"), None, None), P(("gz", "gy"), None, None), P(), P()),
        check_vma=False,
    )
```

time: 758 us -> 77.3 us (0.10); the launches traced: 747 us -> 77 us
  local copies, waits for them, and re-layouts: 344 us -> 8.27 us
  other arithmetic: 155 us -> 0 us
  waiting for transfers between devices: 147 us -> 0 us
  Pallas kernels: 0 us -> 68.1 us
  starting transfers between devices: 59.5 us -> 0 us
  matrix products: 24.7 us -> 0 us
  between operations: 17.5 us -> 0.64 us
    psum x1 -> x0, waiting for transfers between devices: 143 us -> none  [shards(): w_sub_sum, w_down_sum = lax.psum((w_sub_part, w_down_part), ('gz', 'gy'))]
    gather x99 -> x0, local copies, waits for them, and re-layouts: 103 us -> none  [the longest x36 29.3 us: build_padded(): remote = z_faces[side_z][:, :, from_y, from_x][chosen][:, :, None]]
    squeeze x30 -> x0, local copies, waits for them, and re-layouts: 72.2 us -> none  [the longest x4 43.7 us: build_padded(): portion = nearby[:, column][:, :, from_z, from_y, from_x]]
    slice x66 -> x0, local copies, waits for them, and re-layouts: 70.4 us -> none  [the longest x12 25 us: build_padded(): remote = y_faces[side_y][:, :, from_z, from_x][chosen][:, :, :, None]]
    pallas_call x0 -> x1, Pallas kernels: none -> 68.1 us  [shards(): pl.pallas_call(functools.partial(body, scale), out_shape=(jax.ShapeDtypeS...]
    unnamed x503 -> x8, local copies, waits for them, and re-layouts: 68.1 us -> 6.34 us
    scatter x48 -> x0, other arithmetic: 61.1 us -> none  [build_padded(): padded = padded.at[:, :, into_z, into_y, into_x].set(portion)]
    ppermute x19 -> x0, starting transfers between devices: 59.4 us -> none  [the longest x8 33 us: padded_2(): lax.ppermute(lax.slice_in_dim(block, block.shape[dim] - width, None, axis...]
  transfers between devices with their start and end apart: 20 -> 0, of which waited for: 2 -> 0; matrix products, arithmetic and copies ran while one was open for 58% -> 0% of each run, Pallas kernels for 0% -> 0%
where the time goes in v1:
time: 77.3 us; the launch traced here: 77 us
  Pallas kernels  68.1 us (88%)
  local copies, waits for them, and re-layouts  8.27 us (11%)
    pallas_call x1, Pallas kernels, shards(): pl.pallas_call(functools.partial(body, scale), out_shape=(jax.ShapeDtypeS...  68.1 us
    unnamed x8, local copies, waits for them, and re-layouts  6.34 us
    pallas_call x1, local copies, waits for them, and re-layouts, shards(): pl.pallas_call(functools.partial(body, scale), out_shape=(jax.ShapeDtypeS...  1.93 us

profile of v1, /device:TPU:1, one launch (start us, length us, event | category | flops | bytes accessed | tf_op | source)
XLA Modules:
  0.0 77.0 jit_solution(2932346552288694229)
XLA Ops:
  0.6 1.7 %copy.21.w_down = bf16[8,128,64]{2,1,0:T(8,128)(2,1)} copy(bf16[8,128,64]{1,2,0:T(8,128)(2,1)} %param.22) | data formatting | bytes 262144 | tf_op args[5]
  2.4 68.1 %sparse_conv.1 = (bf16[8,128,512]{2,1,0:T(8,128)(2,1)}, bf16[8,64,512]{2,1,0:T(8,128)(2,1)}, f32[27,64,64]{2,1,0:T(8,128)}, f32[8,128,64]{2,1,0:T(8,128)}) custom-call(bf16[8,64,512]{2,1,0:T(8,128)(2,1)} %feat.1, s32[8,512]{1,0:T(8,128)} %occ.1, s32[8,27]{1,0:T(8,128)} %nbr.1, s32[1,8]{1,0:T(1,128)} %bitcast.1, s32[1,8]{1,0:T(1,128)} %bitcast.2, ...), custom_call_target="tpu_custom_call" | custom-call | flops 6000000000 | bytes 12000000 | tf_op jit(solution)/shard_map/sparse_conv/pallas_call | solution.py:586
  70.5 1.9 %copy.22 = f32[8,128,64]{1,2,0:T(8,128)} copy(f32[8,128,64]{2,1,0:T(8,128)} %get-tuple-element.7) | data formatting | bytes 524288 | tf_op jit(solution)/shard_map/sparse_conv/pallas_call | solution.py:586
  72.5 0.0 copy-start.1
  72.5 2.3 %copy.26 = bf16[8,128,512]{2,1,0:T(8,128)(2,1)} copy(bf16[8,128,512]{2,1,0:T(8,128)(2,1)} %get-tuple-element.12) | data formatting | bytes 2097152
  74.8 0.0 copy-done.1
  74.8 0.0 copy-start
  74.8 0.8 %copy.27 = bf16[8,64,512]{2,1,0:T(8,128)(2,1)} copy(bf16[8,64,512]{2,1,0:T(8,128)(2,1)S(1)} %copy-done.1) | data formatting | bytes 1048576
  75.6 0.6 copy-done
  76.1 0.9 %copy.28 = f32[27,64,64]{2,1,0:T(8,128)} copy(f32[27,64,64]{2,1,0:T(8,128)S(1)} %copy-done) | data formatting | bytes 884736
Async XLA Ops:
  72.5 2.3 %copy-start.1 = (bf16[8,64,512]{2,1,0:T(8,128)(2,1)S(1)}, bf16[8,64,512]{2,1,0:T(8,128)(2,1)}, u32[]{:S(2)}) copy-start(bf16[8,64,512]{2,1,0:T(8,128)(2,1)} %get-tuple-element.13) | copy-start | bytes 1572868
  74.8 1.4 %copy-start = (f32[27,64,64]{2,1,0:T(8,128)S(1)}, f32[27,64,64]{2,1,0:T(8,128)}, u32[]{:S(2)}) copy-start(f32[27,64,64]{2,1,0:T(8,128)} %get-tuple-element.14) | copy-start | bytes 1327108

commit v2 on v1

v2 whole, which is shorter than its diff:
```python
import functools

import jax
import jax.numpy as jnp
import numpy as np
from jax import lax
from jax.experimental import pallas as pl
from jax.experimental.pallas import tpu as pltpu
from jax.sharding import PartitionSpec as P

MESH = pl.DeviceIdType.MESH
BF = jnp.bfloat16
F32 = jnp.float32

Y_LOW, Y_HIGH, ZERO, Z_LOW, Z_HIGH, DIAGONAL, BANK = 64, 128, 192, 200, 208, 216, 248


def one_hot(shape, pairs):
    out = np.zeros(shape, np.float32)
    for row, column in pairs:
        out[row, column] = 1.0
    return jnp.asarray(out, BF)


def lane(y, x):
    return 10 * (y + 1) + x + 1


def permutations():
    wrap = [
        (64 * h + 8 * ((yp - 1) % 8) + (xp - 1) % 8, 128 * h + 10 * yp + xp)
        for h in range(2) for yp in range(10) for xp in range(10)
    ]
    rewrap = [
        (lane((yp - 1) % 8, (xp - 1) % 8), 10 * yp + xp) for yp in range(10) for xp in range(10)
    ]
    native = [
        (128 * h + lane(y, x), 64 * h + 8 * y + x)
        for h in range(2) for y in range(8) for x in range(8)
    ]
    pack = [
        (128 * z + 90 * side + x + 1, 64 * side + 8 * z + x)
        for side in range(2) for z in range(8) for x in range(8)
    ]
    unpack = [
        [
            (64 * parity + 8 * z + (xp - 1) % 8, 1024 * parity + 128 * z + 90 * side + xp)
            for parity in range(2) for z in range(8) for xp in range(10)
        ]
        for side in range(2)
    ]
    phase, octant = [], []
    for z in range(8):
        for y in range(8):
            for x in range(8):
                k = 4 * (z % 2) + 2 * (y % 2) + x % 2
                v = 16 * (z // 2) + 4 * (y // 2) + x // 2
                phase.append((128 * z + lane(y, x), 64 * k + v))
                k = 4 * (z // 4) + 2 * (y // 4) + x // 4
                v = 16 * (z % 4) + 4 * (y % 4) + x % 4
                octant.append((64 * k + v, 64 * z + 8 * y + x))
    flip = lambda pairs: [(b, a) for a, b in pairs]
    return (
        one_hot((128, 256), wrap),
        one_hot((128, 128), rewrap),
        one_hot((256, 128), native),
        one_hot((1024, 128), pack),
        one_hot((128, 2048), unpack[0]),
        one_hot((128, 2048), unpack[1]),
        one_hot((1024, 512), phase),
        one_hot((512, 1024), flip(phase)),
        one_hot((512, 512), octant),
        one_hot((512, 512), flip(octant)),
    )


def dot(a, b):
    return jnp.dot(a, b, preferred_element_type=F32)


def dot_nt(a, b):
    return lax.dot_general(a, b, (((1,), (1,)), ((), ())), preferred_element_type=F32)


def roll(x, shift):
    return pltpu.roll(x, shift % 128, x.ndim - 1)


PERMUTATIONS = ("wrap", "rewrap", "native", "pack", "un0", "un1", "phase", "unphase", "oct", "unoct")


def body(scale, *refs):
    operands, results, scratch = refs[:17], refs[17:21], refs[21:]
    nbr_h, occ_h, feat_h, dest_h, w_sub_h, w_down_h, cgrad = operands[:7]
    coarse, feat_grad, ws_out, wd_out = results
    nbr, occ, feat, dest_v, dest_s, w_sub, w_down = scratch[:7]
    p_wrap, p_rewrap, p_native, p_pack, p_un0, p_un1, p_phase, p_unphase, p_oct, p_unoct = scratch[7:17]
    (
        bank1, bank2, ysend, ydst, zsend, dsend, drecv, idx_v, idx_s, inv_v, inv_s, dest_buf, dest_in,
        cg_bank, og_in, og_all, og, ag_ph, ag, occ_p, r0, r1, act, phases, pg, wf, wb, wd, wdt,
        bl, bl_in, bl_bank, fg, wg, coarse_v, feat_v, ws_v,
        src, rc, s1, t1, t2, t3, fin, wd_v,
        h_send, h_recv, c_send, c_recv, in_sem, idx_sem, out_sem, r_send, r_recv,
    ) = scratch[17:]
    gz, gy = lax.axis_index("gz"), lax.axis_index("gy")
    cy, cz, core = gz // 8, (gz // 2) % 4, gz % 2
    nz, ny = 32, 4

    def at(dz, dy):
        return {"gz": (gz + dz + nz) % nz, "gy": (gy + dy + ny) % ny}

    def along(axis, d):
        if axis == 0:
            return {"gz": gz, "gy": (gy + d) % 4}
        if axis == 1:
            return {"gz": ((cy + d) % 4 * 4 + cz) * 2 + core, "gy": gy}
        return {"gz": (cy * 4 + (cz + d) % 4) * 2 + core, "gy": gy}

    coordinate = (gy, cy, cz)
    partner = {"gz": gz + 1 - 2 * core, "gy": gy}
    halo_steps = [(dz, dy) for dz in (-1, 0, 1) for dy in (-1, 0, 1) if (dz, dy) != (0, 0)]
    barrier = pltpu.get_barrier_semaphore()
    greeted = [at(*s) for s in halo_steps] + [partner]
    greeted += [along(axis, d) for axis in range(3) for d in (1, 2, 3)]
    for device in greeted:
        pl.semaphore_signal(barrier, inc=1, device_id=device, device_id_type=MESH)

    loads = {}

    def load(name, source, target):
        loads[name] = pltpu.make_async_copy(source, target, in_sem.at[len(loads)])
        loads[name].start()

    permuting = dict(zip(PERMUTATIONS, zip(operands[7:], scratch[7:17])))
    load("feat", feat_h, feat)
    load("occ", occ_h, occ)
    load("wrap", *permuting["wrap"])
    load("nbr", nbr_h, nbr)
    load("dest", dest_h, dest_v)
    load("dest_s", dest_h, dest_s)
    load("pack", *permuting["pack"])
    load("w_sub", w_sub_h, w_sub)
    load("w_down", w_down_h, w_down)
    load("cgrad", cgrad, cg_bank.at[pl.ds(0, 8)])
    for name in ("unoct", "unphase", "un0", "un1", "rewrap", "phase", "native", "oct"):
        load(name, *permuting[name])

    def send(src, dst, send_sem, recv_sem, device):
        copy = pltpu.make_async_remote_copy(
            src_ref=src, dst_ref=dst, send_sem=send_sem, recv_sem=recv_sem,
            device_id=device, device_id_type=MESH,
        )
        copy.start()
        return copy

    lanes = lax.broadcasted_iota(jnp.int32, (64, 128), 1)
    low_half = lax.broadcasted_iota(jnp.int32, (128, 128), 1) < 64
    xp = lanes - 10 * lax.shift_right_logical(lanes * 205, 11)
    first, last = xp == 0, xp == 9
    low64 = lanes < 64
    yp_low, yp_high = lanes < 10, lanes >= 90
    center_row = lax.broadcasted_iota(jnp.int32, (8, 128), 1)
    center_x = center_row - 10 * lax.shift_right_logical(center_row * 205, 11)
    center = (center_row > 10) & (center_row < 89) & (center_x > 0) & (center_x < 9)

    loads["nbr"].wait()
    table = nbr[...]
    owner = table // 8
    slot = table - owner * 8
    step_z = owner // 4 - gz
    step_y = owner - owner // 4 * 4 - gy
    column = lax.broadcasted_iota(jnp.int32, (8, 27), 1)
    part_a = column // 9
    edge_z = jnp.where(part_a == 0, 7, 0)
    on_z = Z_LOW + jnp.where(step_z > 0, 8, 0) + slot
    on_diagonal = DIAGONAL + jnp.where(step_z > 0, 16, 0) + jnp.where(step_y > 0, 8, 0) + slot
    same_z = jnp.where(step_y == 0, 0, jnp.where(step_y < 0, Y_LOW, Y_HIGH)) + slot * 8 + edge_z
    index = jnp.where(step_z == 0, same_z, jnp.where(step_y == 0, on_z, on_diagonal))
    index = jnp.where((table < 0) | ((part_a == 1) & (index > ZERO)), ZERO, index)
    idx_v[...] = jnp.zeros_like(idx_v)
    idx_v[:, 0:27] = index
    idx_copy = pltpu.make_async_copy(idx_v, idx_s, idx_sem.at[0])
    idx_copy.start()

    loads["feat"].wait()
    loads["occ"].wait()
    loads["wrap"].wait()
    for q in range(4):
        part = feat[:, :, 128 * q:128 * q + 128]
        flag = occ[:, 128 * q:128 * q + 128].astype(F32).astype(BF)
        rows = [part[t] * flag[t:t + 1] for t in range(8)]
        planes = dot(jnp.concatenate(rows, axis=0), p_wrap[...]).astype(BF)
        flags = dot(flag, p_wrap[...])
        for h in range(2):
            flag_plane = jnp.where(center, flags[:, 128 * h:128 * h + 128], 0.0)
            for t in range(8):
                occ_p[t, :, 128 * (2 * q + h):128 * (2 * q + h) + 128] = flag_plane[t:t + 1]
                bank1[8 * t + 2 * q + h] = planes[64 * t:64 * t + 64, 128 * h:128 * h + 128]

    loads["dest"].wait()
    dest_buf[0] = jnp.zeros((8, 128), jnp.int32) - 1
    dest_buf[0, 0:1, 0:8] = dest_v[...]
    for bank in (bank1, bank2):
        bank[ZERO:ZERO + 8] = jnp.zeros((8, 64, 128), BF)
    loads["pack"].wait()

    pl.semaphore_wait(barrier, len(greeted))
    dest_send = send(dest_buf.at[0], dest_buf.at[1], c_send.at[0], c_recv.at[0], partner)
    cg_send = send(cgrad, cg_bank.at[pl.ds(8, 8)], c_send.at[1], c_recv.at[1], partner)

    def publish(bank, which):
        copies = []
        total = None
        for q in range(4):
            both = jnp.concatenate(
                [
                    jnp.concatenate([bank[8 * t + 2 * q], bank[8 * t + 2 * q + 1]], axis=1)
                    for t in range(8)
                ],
                axis=0,
            )
            term = dot(both, p_pack[256 * q:256 * q + 256, :])
            total = term if total is None else total + term
        for j in range(4):
            even, odd = total[128 * j:128 * j + 64], total[128 * j + 64:128 * j + 128]
            ysend[which, 0, j] = jnp.where(low64, even, roll(odd, 64)).astype(BF)
            ysend[which, 1, j] = jnp.where(low64, roll(even, 64), odd).astype(BF)
        for side in range(2):
            for t in range(8):
                zsend[which, side, t] = bank[8 * t + (7 if side == 0 else 0)]
        for side in range(2):
            up = 1 - 2 * side
            copies.append(
                send(
                    ysend.at[which, side], ydst.at[which, side],
                    h_send.at[which, side], h_recv.at[which, side], at(0, up),
                )
            )
            copies.append(
                send(
                    zsend.at[which, side], bank.at[pl.ds(Z_LOW if side == 0 else Z_HIGH, 8)],
                    h_send.at[which, 2 + side], h_recv.at[which, 2 + side], at(up, 0),
                )
            )
        for side_z in range(2):
            for side_y in range(2):
                number = 2 * side_z + side_y
                gathered = None
                for t in range(8):
                    piece = bank[8 * t + (7 if side_z == 0 else 0)].astype(F32)
                    piece = roll(piece, 16 * t - 90 * side_y)
                    piece = jnp.where((lanes >= 16 * t) & (lanes < 16 * t + 10), piece, 0.0)
                    gathered = piece if gathered is None else gathered + piece
                dsend[which, number] = gathered.astype(BF)
                copies.append(
                    send(
                        dsend.at[which, number], drecv.at[which, number],
                        h_send.at[which, 4 + number], h_recv.at[which, 4 + number],
                        at(1 - 2 * side_z, 1 - 2 * side_y),
                    )
                )
        return copies

    def receive(bank, which, copies):
        for copy in copies:
            copy.wait_recv()
        for side in range(2):
            rows = ydst[which, side].reshape(256, 128)
            for q in range(8):
                planes = dot(rows, (p_un0, p_un1)[side][:, 256 * q:256 * q + 256]).astype(BF)
                for j in range(4):
                    for h in range(2):
                        t, z = 2 * j + q // 4, 2 * (q % 4) + h
                        bank[(Y_LOW, Y_HIGH)[side] + 8 * t + z] = planes[
                            64 * j:64 * j + 64, 128 * h:128 * h + 128
                        ]
        for side_z in range(2):
            for side_y in range(2):
                number = 2 * side_z + side_y
                packed = drecv[which, number].astype(F32)
                for t in range(8):
                    bank[DIAGONAL + 8 * number + t] = roll(packed, 90 * side_y - 16 * t).astype(BF)

    def assemble(bank, t, r_buf, i, planes):
        for zp in planes:
            a = 0 if zp == 0 else (2 if zp == 9 else 1)
            rows = []
            for b in range(3):
                loaded = []
                for c in range(3):
                    place = idx_s[t, 9 * a + 3 * b + c] + (zp - 1 if a == 1 else 0)
                    loaded.append(bank[place])
                rows.append(jnp.where(first, loaded[0], jnp.where(last, loaded[2], loaded[1])))
            plane = jnp.where(yp_low, rows[0], jnp.where(yp_high, rows[2], rows[1]))
            wide = plane.astype(F32)
            columns = slice(128 * zp, 128 * zp + 128)
            r_buf[i, 0:64, columns] = roll(wide, 10).astype(BF)
            r_buf[i, 64:128, columns] = plane
            r_buf[i, 128:192, columns] = roll(wide, -10).astype(BF)

    def convolve(weights, r_buf, i, q):
        total = None
        for a in range(3):
            term = dot(weights[a], r_buf[i, :, 128 * a + 256 * q:128 * a + 256 * q + 256])
            total = term if total is None else total + term
        parts = []
        for h in range(2):
            y = total[:, 128 * h:128 * h + 128]
            parts.append(roll(y[0:64], 1) + y[64:128] + roll(y[128:192], -1))
        return parts

    groups = ((0, 1, 2), (3, 4, 5), (6, 7), (8, 9))

    def sweep(bank, low, high, tile):
        if low == 0:
            for planes in groups:
                assemble(bank, 0, r0, 0, planes)

        @pl.loop(low, high)
        def _(i):
            for q in range(4):
                assemble(bank, 2 * i + 1, r1, i, groups[q])
                tile(r0, i, 2 * i, q)
            for q in range(4):
                assemble(bank, jnp.minimum(2 * i + 2, 7), r0, i + 1, groups[q])
                tile(r1, i, 2 * i + 1, q)

    halo = publish(bank1, 0)

    loads["w_sub"].wait()
    loads["w_down"].wait()
    for a in range(3):
        for c in range(3):
            wf[a, 64 * c:64 * c + 64, :] = jnp.concatenate(
                [w_sub[9 * a + 3 * b + c].astype(F32) for b in range(3)], axis=1
            ).astype(BF)
        turned = jnp.concatenate(
            [
                jnp.concatenate(
                    [w_sub[9 * (2 - a) + 3 * (2 - b) + 2 - c].astype(F32) for c in range(3)], axis=1
                )
                for b in range(3)
            ],
            axis=0,
        )
        wb[a] = turned.T.astype(BF)
    wdt[...] = w_down[...].reshape(512, 128)
    wd[...] = wdt[...].astype(F32).T.astype(BF)

    cg_bank[16] = jnp.zeros((128, 512), BF)
    idx_copy.wait()
    loads["dest_s"].wait()
    loads["cgrad"].wait()
    loads["unoct"].wait()
    cg_send.wait_recv()
    base = gz * 4 + gy
    partner_index = (gz + 1 - 2 * core) * 4 + gy
    for t in range(8):
        d = dest_s[0, t]
        own = d // 8 - base * 8
        other = d // 8 - partner_index * 8
        chosen = jnp.where((other >= 0) & (other < 8), 8 + other, 16)
        chosen = jnp.where((own >= 0) & (own < 8), own, chosen)
        og_in[128 * t:128 * t + 128, :] = cg_bank[chosen]
    for q in range(2):
        split = dot(og_in[...], p_unoct[:, 256 * q:256 * q + 256]).astype(BF)
        for t in range(8):
            for h in range(2):
                og_all[4 * t + 2 * q + h] = split[128 * t:128 * t + 128, 128 * h:128 * h + 128]
    for j in range(4):
        halves = []
        for h in range(2):
            t = 2 * j + h
            d = dest_s[0, t]
            octant = d - d // 8 * 8
            piece = og_all[4 * t + octant // 2].astype(F32)
            odd = octant - octant // 2 * 2
            halves.append(jnp.where(odd == h, piece, roll(piece, 64)))
        og[:, 128 * j:128 * j + 128] = jnp.where(low_half, halves[0], halves[1]).astype(BF)
    for r in range(4):
        rows = dot(wdt[128 * r:128 * r + 128, :], og[...]).astype(BF).astype(F32)
        for j in range(4):
            even = rows[0:64, 128 * j:128 * j + 128]
            odd = rows[64:128, 128 * j:128 * j + 128]
            columns = slice(128 * r, 128 * r + 128)
            ag_ph[128 * j:128 * j + 64, columns] = jnp.where(low64, even, roll(odd, 64)).astype(BF)
            ag_ph[128 * j + 64:128 * j + 128, columns] = jnp.where(
                low64, roll(even, 64), odd
            ).astype(BF)
    loads["unphase"].wait()
    for q in range(4):
        spread = dot(ag_ph[...], p_unphase[:, 256 * q:256 * q + 256]).astype(BF)
        for t in range(8):
            ag[t, :, 256 * q:256 * q + 256] = spread[64 * t:64 * t + 64]

    dest_send.wait_recv()
    dest_copy = pltpu.make_async_copy(dest_buf.at[1], dest_in, idx_sem.at[2])
    dest_copy.start()
    dest_copy.wait()
    place = lax.broadcasted_iota(jnp.int32, (8, 128), 1) + base * 64
    inverse = jnp.zeros((8, 128), jnp.int32) + 16
    for s in range(8):
        inverse = jnp.where(place == dest_s[0, s], s, inverse)
        inverse = jnp.where(place == dest_in[0, s], 8 + s, inverse)
    inv_v[...] = inverse
    inv_copy = pltpu.make_async_copy(inv_v, inv_s, idx_sem.at[3])
    inv_copy.start()

    loads["un0"].wait()
    loads["un1"].wait()
    receive(bank1, 0, halo)

    def forward(r_buf, i, t, q):
        parts = convolve(wf, r_buf, i, q)
        for h in range(2):
            z = 2 * q + h
            v = parts[h]
            on = occ_p[t, :, 128 * z:128 * z + 128]
            s = 1.0 / (1.0 + jnp.exp(-v))
            act[t, :, 128 * z:128 * z + 128] = jnp.where(on > 0.5, v * s, 0.0).astype(BF)
            g = ag[t, :, 128 * z:128 * z + 128].astype(F32)
            g = g * s * (1.0 + v * (1.0 - s))
            pg[8 * t + z] = jnp.where(on > 0.5, g, 0.0).astype(BF)

    sweep(bank1, 0, 4, forward)

    wg[...] = jnp.zeros_like(wg)

    @pl.loop(0, 4)
    def _(i):
        for h in range(2):
            planes = [pg[8 * (2 * i + h) + z].astype(F32) for z in range(8)]
            shifted = jnp.concatenate(
                [
                    jnp.concatenate([roll(p, c - 1).astype(BF) for p in planes], axis=1)
                    for c in range(3)
                ],
                axis=0,
            )
            for a in range(3):
                wg[a] += dot_nt(shifted, (r0, r1)[h][i, :, 128 * a:128 * a + 1024])

    for a in range(3):
        src[192 * a:192 * a + 192, :] = wg[a, :, 0:128]
    src[576:768, :] = jnp.concatenate([wg[0, :, 128:192], wg[1, :, 128:192]], axis=1)
    src[768:960, 0:64] = wg[2, :, 128:192]
    src[768:960, 64:128] = jnp.zeros((192, 64), F32)

    loads["phase"].wait()
    for q in range(2):
        split = dot(act[...].reshape(512, 1024), p_phase[:, 256 * q:256 * q + 256])
        for j in range(4):
            for h in range(2):
                even = split[128 * j:128 * j + 64, 128 * h:128 * h + 128]
                odd = split[128 * j + 64:128 * j + 128, 128 * h:128 * h + 128]
                k = 4 * q + 2 * h
                columns = slice(128 * j, 128 * j + 128)
                phases[64 * k:64 * k + 64, columns] = jnp.where(
                    low64, even, roll(odd, 64)
                ).astype(BF)
                phases[64 * k + 64:64 * k + 128, columns] = jnp.where(
                    low64, roll(even, 64), odd
                ).astype(BF)
    src[960:1472, :] = dot_nt(phases[...], og[...])
    src[1472:1536, :] = jnp.zeros((64, 128), F32)

    reduced = []

    def pair(n):
        return r_send.at[n], r_recv.at[n]

    def rows_at(start, size):
        return pl.ds(pl.multiple_of(start, 8), size)

    def axis_of(p, stage):
        return (p + stage) % 3

    def me(p, stage):
        return coordinate[axis_of(p, stage)]

    def stage_0():
        return [
            [send(src.at[rows_at(768 * (1 - core) + 256 * p, 256)], rc.at[p], *pair(p), partner)]
            for p in range(3)
        ]

    def arrived(copies):
        for copy in copies:
            copy.wait_recv()

    def stage_1(before):
        out = []
        for p in range(3):
            arrived(before[p])
            s1[p] = src[rows_at(768 * core + 256 * p, 256)] + rc[p]
            copies = []
            for d in (1, 2, 3):
                to = (me(p, 0) + d) % 4
                copies.append(
                    send(
                        s1.at[p, rows_at(64 * to, 64)], t1.at[p, d - 1],
                        *pair(3 + 3 * p + d - 1), along(axis_of(p, 0), d),
                    )
                )
            out.append(copies)
        return out

    def stage_2(before):
        out = []
        for p in range(3):
            arrived(before[p])
            total = s1[p, rows_at(64 * me(p, 0), 64)]
            for d in range(3):
                total = total + t1[p, d]
            out.append(exchange(t2, p, 1, total, 12))
        return out

    def exchange(buffer, p, stage, value, first_pair):
        buffer[p, me(p, stage)] = value
        place = buffer.at[p, me(p, stage)]
        return [
            send(place, place, *pair(first_pair + 3 * p + d - 1), along(axis_of(p, stage), d))
            for d in (1, 2, 3)
        ]

    def stage_3(before):
        out = []
        for p in range(3):
            arrived(before[p])
            total = (t2[p, 0] + t2[p, 1]) + (t2[p, 2] + t2[p, 3])
            out.append(exchange(t3, p, 2, total, 21))
        return out

    def stage_4(before):
        out = []
        for p in range(3):
            arrived(before[p])
            rows = rows_at(768 * core + 256 * p + 64 * me(p, 0), 64)
            total = (t3[p, 0] + t3[p, 1]) + (t3[p, 2] + t3[p, 3])
            fin[rows] = (total * scale).astype(BF)
            out.append(
                [
                    send(fin.at[rows], fin.at[rows], *pair(30 + 3 * p + d - 1), along(axis_of(p, 0), d))
                    for d in (1, 2, 3)
                ]
            )
        return out

    def stage_5(before):
        out = []
        for p in range(3):
            arrived(before[p])
            rows = rows_at(768 * core + 256 * p, 256)
            out.append([send(fin.at[rows], fin.at[rows], *pair(39 + p), partner)])
        return out

    stages = [stage_0, stage_1, stage_2, stage_3, stage_4, stage_5]

    def reduce_step():
        n = len(reduced)
        reduced.append(stages[n](reduced[-1]) if n > 0 else stages[0]())

    reduce_step()

    loads["rewrap"].wait()
    for t in range(8):
        rows = pg[8 * t:8 * t + 8].reshape(512, 128)
        bank2[8 * t:8 * t + 8] = dot(rows, p_rewrap[...]).astype(BF).reshape(8, 64, 128)

    halo2 = publish(bank2, 1)

    bl[...] = dot(wd[...], phases[...]).astype(BF)
    bl_send = send(bl, bl_in, c_send.at[2], c_recv.at[2], partner)
    reduce_step()
    inv_copy.wait()
    bl_send.wait_recv()
    bl_bank[16] = jnp.zeros((128, 128), BF)
    for source in range(2):
        blocks = (bl, bl_in)[source]
        for j in range(4):
            both = blocks[:, 128 * j:128 * j + 128].astype(F32)
            turned = roll(both, 64)
            bl_bank[8 * source + 2 * j] = jnp.where(low_half, both, turned).astype(BF)
            bl_bank[8 * source + 2 * j + 1] = jnp.where(low_half, turned, both).astype(BF)
    for c in range(8):
        for q in range(4):
            even = bl_bank[inv_s[0, 8 * c + 2 * q]]
            odd = bl_bank[inv_s[0, 8 * c + 2 * q + 1]]
            og_in[128 * c:128 * c + 128, 128 * q:128 * q + 128] = jnp.where(low_half, even, odd)
    loads["oct"].wait()
    for q in range(2):
        rows = dot(og_in[...], p_oct[:, 256 * q:256 * q + 256]).astype(BF)
        coarse_v[:, :, 256 * q:256 * q + 256] = rows.reshape(8, 128, 256)
    coarse_out = pltpu.make_async_copy(coarse_v, coarse, out_sem.at[1])
    coarse_out.start()
    reduce_step()
    reduce_step()
    receive(bank2, 1, halo2)

    def backward(r_buf, i, t, q):
        parts = convolve(wb, r_buf, i, q)
        for h in range(2):
            z = 2 * q + h
            on = occ_p[t, :, 128 * z:128 * z + 128]
            fg[t, :, 128 * z:128 * z + 128] = jnp.where(on > 0.5, parts[h], 0.0).astype(BF)

    sweep(bank2, 0, 2, backward)
    reduce_step()
    sweep(bank2, 2, 4, backward)
    reduce_step()
    loads["native"].wait()
    for q in range(4):
        rows = dot(fg[:, :, 256 * q:256 * q + 256].reshape(512, 256), p_native[...])
        feat_v[:, :, 128 * q:128 * q + 128] = rows.astype(BF).reshape(8, 64, 128)
    feat_out = pltpu.make_async_copy(feat_v, feat_grad, out_sem.at[0])
    feat_out.start()

    for p in range(3):
        arrived(reduced[5][p])
    wd_v[...] = fin[960:1472, :].astype(F32)
    down_out = pltpu.make_async_copy(wd_v, wd_out, out_sem.at[2])
    down_out.start()
    for a in range(3):
        for c in range(3):
            for b in range(2):
                rows = slice(192 * a + 64 * c, 192 * a + 64 * c + 64)
                ws_v[9 * a + 3 * b + c] = fin[rows, 64 * b:64 * b + 64].astype(F32)
            row, column = ((576, 0), (576, 64), (768, 0))[a]
            rows = slice(row + 64 * c, row + 64 * c + 64)
            ws_v[9 * a + 6 + c] = fin[rows, column:column + 64].astype(F32)
    sub_out = pltpu.make_async_copy(ws_v, ws_out, out_sem.at[3])
    sub_out.start()
    for copy in halo + halo2 + [dest_send, cg_send, bl_send]:
        copy.wait_send()
    for stage in reduced:
        for copies in stage:
            for copy in copies:
                copy.wait_send()
    for copy in (feat_out, coarse_out, down_out, sub_out):
        copy.wait()


def shards(features, occupancy, neighbors, coarse_dest, w_sub, w_down, coarse_grad):
    devices = lax.axis_size("gz") * lax.axis_size("gy")
    scale = (features.shape[0] * devices * 512.0) ** -0.5
    anywhere = pl.BlockSpec(memory_space=pl.ANY)
    constants = permutations()
    vmem, smem, dma = pltpu.VMEM, pltpu.SMEM, pltpu.SemaphoreType.DMA
    i32 = jnp.int32
    coarse, feat_grad, ws, wd = pl.pallas_call(
        functools.partial(body, scale),
        out_shape=(
            vmem((8, 128, 512), BF), vmem((8, 64, 512), BF), vmem((27, 64, 64), F32), vmem((512, 128), F32),
        ),
        in_specs=[anywhere] * 17,
        out_specs=(anywhere,) * 4,
        scratch_shapes=[
            vmem((8, 27), i32), vmem((8, 512), i32), vmem((8, 64, 512), BF), vmem((1, 8), i32),
            smem((1, 8), i32), vmem((27, 64, 64), BF), vmem((8, 64, 128), BF),
        ] + [vmem(c.shape, BF) for c in constants] + [
            vmem((BANK, 64, 128), BF), vmem((BANK, 64, 128), BF),
            vmem((2, 2, 4, 64, 128), BF), vmem((2, 2, 4, 64, 128), BF), vmem((2, 2, 8, 64, 128), BF),
            vmem((2, 4, 64, 128), BF), vmem((2, 4, 64, 128), BF),
            vmem((8, 128), i32), smem((8, 128), i32), vmem((8, 128), i32), smem((8, 128), i32),
            vmem((2, 8, 128), i32), smem((8, 128), i32),
            vmem((17, 128, 512), BF), vmem((1024, 512), BF), vmem((32, 128, 128), BF),
            vmem((128, 512), BF), vmem((512, 512), BF), vmem((8, 64, 1024), BF),
            vmem((8, 1, 1024), F32), vmem((5, 192, 1280), BF), vmem((4, 192, 1280), BF),
            vmem((8, 64, 1024), BF), vmem((512, 512), BF), vmem((64, 64, 128), BF),
            vmem((3, 192, 192), BF), vmem((3, 192, 192), BF), vmem((128, 512), BF), vmem((512, 128), BF),
            vmem((128, 512), BF), vmem((128, 512), BF), vmem((17, 128, 128), BF),
            vmem((8, 64, 1024), BF), vmem((3, 192, 192), F32),
            vmem((8, 128, 512), BF), vmem((8, 64, 512), BF), vmem((27, 64, 64), F32),
            vmem((1536, 128), F32), vmem((3, 256, 128), F32), vmem((3, 256, 128), F32),
            vmem((3, 3, 64, 128), F32), vmem((3, 4, 64, 128), F32), vmem((3, 4, 64, 128), F32),
            vmem((1536, 128), BF), vmem((512, 128), F32),
            dma((2, 8)), dma((2, 8)), dma((3,)), dma((3,)), dma((18,)), dma((4,)), dma((4,)),
            dma((42,)), dma((42,)),
        ],
        compiler_params=pltpu.CompilerParams(
            collective_id=0, has_side_effects=True, vmem_limit_bytes=60 * 1024 * 1024
        ),
        cost_estimate=pl.CostEstimate(flops=6 * 10**9, bytes_accessed=12 * 10**6, transcendentals=10**6),
        name="sparse_conv",
    )(
        neighbors, occupancy, features, coarse_dest.reshape(1, 8), w_sub,
        w_down.transpose(0, 2, 1), coarse_grad, *constants,
    )
    return coarse, feat_grad, ws, wd.reshape(8, 64, 128).transpose(0, 2, 1)


def solution(mesh):
    return jax.shard_map(
        shards,
        mesh=mesh,
        in_specs=(
            P(("gz", "gy"), None, None),
            P(("gz", "gy"), None),
            P(("gz", "gy"), None),
            P(("gz", "gy")),
            P(),
            P(),
            P(("gz", "gy"), None, None),
        ),
        out_specs=(P(("gz", "gy"), None, None), P(("gz", "gy"), None, None), P(), P()),
        check_vma=False,
    )
```

time: 77.3 us -> 51.8 us (0.67)
  Pallas kernels: 68.1 us -> 47.7 us
  local copies, waits for them, and re-layouts: 8.27 us -> 3.38 us
    pallas_call x1, Pallas kernels: 68.1 us -> 47.7 us  [shards(): pl.pallas_call(functools.partial(body, scale), out_shape=(vmem((8, 128, 5...]
    unnamed x8 -> x4, local copies, waits for them, and re-layouts: 6.34 us -> 3.38 us
    pallas_call x1 -> x0, local copies, waits for them, and re-layouts: 1.93 us -> none  [shards(): pl.pallas_call(functools.partial(body, scale), out_shape=(jax.ShapeDtypeS...]
where the time goes in v2:
time: 51.8 us; the launch traced here: 51.7 us
  Pallas kernels  47.7 us (92%)
  local copies, waits for them, and re-layouts  3.38 us (7%)
  between operations  0.64 us (1%)
    pallas_call x1, Pallas kernels, shards(): pl.pallas_call(functools.partial(body, scale), out_shape=(vmem((8, 128, 5...  47.7 us
    unnamed x4, local copies, waits for them, and re-layouts  3.38 us

profile of v2, /device:TPU:1, one launch (start us, length us, event | category | flops | bytes accessed | tf_op | source)
XLA Modules:
  0.0 51.7 jit_solution(14165617731908208042)
XLA Ops:
  0.6 47.7 %sparse_conv.1 = (bf16[8,128,512]{2,1,0:T(8,128)(2,1)S(1)}, bf16[8,64,512]{2,1,0:T(8,128)(2,1)S(1)}, f32[27,64,64]{2,1,0:T(8,128)S(1)}, f32[512,128]{1,0:T(8,128)S(1)}) custom-call(s32[8,27]{1,0:T(8,128)} %refs_0_.1, s32[8,512]{1,0:T(8,128)} %refs_1_.1, bf16[8,64,512]{2,1,0:T(8,128)(2,1)} %refs_2_.1, s32[1,8]{1,0:T(1,128)} %bitcast.7, ...), custom_call_target="tpu_custom_call" | custom-call | flops 6000000000 | bytes 12000000 | tf_op jit(solution)/shard_map/sparse_conv/pallas_call | solution.py:650
  48.3 1.0 %copy.25 = bf16[8,128,512]{2,1,0:T(8,128)(2,1)} copy(bf16[8,128,512]{2,1,0:T(8,128)(2,1)S(1)} %get-tuple-element.12) | data formatting | bytes 2097152
  49.3 0.7 %copy.28 = f32[8,128,64]{1,2,0:T(8,128)} copy(f32[8,128,64]{1,2,0:T(8,128)S(1)} %bitcast.5) | data formatting | bytes 524288
  50.0 0.8 %copy.26 = bf16[8,64,512]{2,1,0:T(8,128)(2,1)} copy(bf16[8,64,512]{2,1,0:T(8,128)(2,1)S(1)} %get-tuple-element.13) | data formatting | bytes 1048576
  50.8 0.9 %copy.27 = f32[27,64,64]{2,1,0:T(8,128)} copy(f32[27,64,64]{2,1,0:T(8,128)S(1)} %get-tuple-element.14) | data formatting | bytes 884736

commit v3 on v2

--- a/solution.py
+++ b/solution.py
@@ -445,6 +445,87 @@
     src[576:768, :] = jnp.concatenate([wg[0, :, 128:192], wg[1, :, 128:192]], axis=1)
     src[768:960, 0:64] = wg[2, :, 128:192]
     src[768:960, 64:128] = jnp.zeros((192, 64), F32)
+    src[960:1024, :] = jnp.zeros((64, 128), F32)
+
+
+    def pair(n):
+        return r_send.at[n], r_recv.at[n]
+
+    def rows_at(start, size):
+        return pl.ds(pl.multiple_of(start, 8), size)
+
+    def axis_of(p, stage):
+        return (p + stage) % 3
+
+    def me(p, stage):
+        return coordinate[axis_of(p, stage)]
+
+    def first_row(p, half):
+        return 512 * half + 256 * p if p < 2 else 1024 + 256 * half
+
+    def stage_0(p, _):
+        rows = rows_at(first_row(p, 1 - core), 256)
+        return [send(src.at[rows], rc.at[p], *pair(p), partner)]
+
+    def arrived(copies):
+        for copy in copies:
+            copy.wait_recv()
+
+    def stage_1(p, before):
+        arrived(before)
+        s1[p] = src[rows_at(first_row(p, core), 256)] + rc[p]
+        copies = []
+        for d in (1, 2, 3):
+            to = (me(p, 0) + d) % 4
+            copies.append(
+                send(
+                    s1.at[p, rows_at(64 * to, 64)], t1.at[p, d - 1],
+                    *pair(3 + 3 * p + d - 1), along(axis_of(p, 0), d),
+                )
+            )
+        return copies
+
+    def exchange(buffer, p, stage, value, first_pair):
+        buffer[p, me(p, stage)] = value
+        place = buffer.at[p, me(p, stage)]
+        return [
+            send(place, place, *pair(first_pair + 3 * p + d - 1), along(axis_of(p, stage), d))
+            for d in (1, 2, 3)
+        ]
+
+    def stage_2(p, before):
+        arrived(before)
+        total = s1[p, rows_at(64 * me(p, 0), 64)]
+        for d in range(3):
+            total = total + t1[p, d]
+        return exchange(t2, p, 1, total, 12)
+
+    def stage_3(p, before):
+        arrived(before)
+        return exchange(t3, p, 2, (t2[p, 0] + t2[p, 1]) + (t2[p, 2] + t2[p, 3]), 21)
+
+    def stage_4(p, before):
+        arrived(before)
+        rows = rows_at(first_row(p, core) + 64 * me(p, 0), 64)
+        total = (t3[p, 0] + t3[p, 1]) + (t3[p, 2] + t3[p, 3])
+        fin[rows] = (total * scale).astype(BF)
+        return [
+            send(fin.at[rows], fin.at[rows], *pair(30 + 3 * p + d - 1), along(axis_of(p, 0), d))
+            for d in (1, 2, 3)
+        ]
+
+    def stage_5(p, before):
+        arrived(before)
+        rows = rows_at(first_row(p, core), 256)
+        return [send(fin.at[rows], fin.at[rows], *pair(39 + p), partner)]
+
+    stages = [stage_0, stage_1, stage_2, stage_3, stage_4, stage_5]
+    reduced = [[], [], []]
+
+    def reduce_step(*parts):
+        for p in parts:
+            n = len(reduced[p])
+            reduced[p].append(stages[n](p, reduced[p][-1] if n > 0 else None))
 
     loads["phase"].wait()
     for q in range(2):
@@ -461,117 +542,20 @@
                 phases[64 * k + 64:64 * k + 128, columns] = jnp.where(
                     low64, roll(even, 64), odd
                 ).astype(BF)
-    src[960:1472, :] = dot_nt(phases[...], og[...])
-    src[1472:1536, :] = jnp.zeros((64, 128), F32)
-
-    reduced = []
-
-    def pair(n):
-        return r_send.at[n], r_recv.at[n]
-
-    def rows_at(start, size):
-        return pl.ds(pl.multiple_of(start, 8), size)
-
-    def axis_of(p, stage):
-        return (p + stage) % 3
-
-    def me(p, stage):
-        return coordinate[axis_of(p, stage)]
-
-    def stage_0():
-        return [
-            [send(src.at[rows_at(768 * (1 - core) + 256 * p, 256)], rc.at[p], *pair(p), partner)]
-            for p in range(3)
-        ]
-
-    def arrived(copies):
-        for copy in copies:
-            copy.wait_recv()
-
-    def stage_1(before):
-        out = []
-        for p in range(3):
-            arrived(before[p])
-            s1[p] = src[rows_at(768 * core + 256 * p, 256)] + rc[p]
-            copies = []
-            for d in (1, 2, 3):
-                to = (me(p, 0) + d) % 4
-                copies.append(
-                    send(
-                        s1.at[p, rows_at(64 * to, 64)], t1.at[p, d - 1],
-                        *pair(3 + 3 * p + d - 1), along(axis_of(p, 0), d),
-                    )
-                )
-            out.append(copies)
-        return out
-
-    def stage_2(before):
-        out = []
-        for p in range(3):
-            arrived(before[p])
-            total = s1[p, rows_at(64 * me(p, 0), 64)]
-            for d in range(3):
-                total = total + t1[p, d]
-            out.append(exchange(t2, p, 1, total, 12))
-        return out
-
-    def exchange(buffer, p, stage, value, first_pair):
-        buffer[p, me(p, stage)] = value
-        place = buffer.at[p, me(p, stage)]
-        return [
-            send(place, place, *pair(first_pair + 3 * p + d - 1), along(axis_of(p, stage), d))
-            for d in (1, 2, 3)
-        ]
-
-    def stage_3(before):
-        out = []
-        for p in range(3):
-            arrived(before[p])
-            total = (t2[p, 0] + t2[p, 1]) + (t2[p, 2] + t2[p, 3])
-            out.append(exchange(t3, p, 2, total, 21))
-        return out
-
-    def stage_4(before):
-        out = []
-        for p in range(3):
-            arrived(before[p])
-            rows = rows_at(768 * core + 256 * p + 64 * me(p, 0), 64)
-            total = (t3[p, 0] + t3[p, 1]) + (t3[p, 2] + t3[p, 3])
-            fin[rows] = (total * scale).astype(BF)
-            out.append(
-                [
-                    send(fin.at[rows], fin.at[rows], *pair(30 + 3 * p + d - 1), along(axis_of(p, 0), d))
-                    for d in (1, 2, 3)
-                ]
-            )
-        return out
-
-    def stage_5(before):
-        out = []
-        for p in range(3):
-            arrived(before[p])
-            rows = rows_at(768 * core + 256 * p, 256)
-            out.append([send(fin.at[rows], fin.at[rows], *pair(39 + p), partner)])
-        return out
-
-    stages = [stage_0, stage_1, stage_2, stage_3, stage_4, stage_5]
-
-    def reduce_step():
-        n = len(reduced)
-        reduced.append(stages[n](reduced[-1]) if n > 0 else stages[0]())
-
-    reduce_step()
+    src[1024:1536, :] = dot_nt(phases[...], og[...])
+
+    reduce_step(0, 1, 2)
+    bl[...] = dot(wd[...], phases[...]).astype(BF)
+    bl_send = send(bl, bl_in, c_send.at[2], c_recv.at[2], partner)
 
     loads["rewrap"].wait()
     for t in range(8):
         rows = pg[8 * t:8 * t + 8].reshape(512, 128)
         bank2[8 * t:8 * t + 8] = dot(rows, p_rewrap[...]).astype(BF).reshape(8, 64, 128)
 
+    reduce_step(0, 1, 2)
     halo2 = publish(bank2, 1)
 
-    bl[...] = dot(wd[...], phases[...]).astype(BF)
-    bl_send = send(bl, bl_in, c_send.at[2], c_recv.at[2], partner)
-    reduce_step()
     inv_copy.wait()
     bl_send.wait_recv()
     bl_bank[16] = jnp.zeros((128, 128), BF)
@@ -593,9 +577,9 @@
         coarse_v[:, :, 256 * q:256 * q + 256] = rows.reshape(8, 128, 256)
     coarse_out = pltpu.make_async_copy(coarse_v, coarse, out_sem.at[1])
     coarse_out.start()
-    reduce_step()
-    reduce_step()
+    reduce_step(0, 1, 2)
     receive(bank2, 1, halo2)
+    reduce_step(0, 1, 2)
 
     def backward(r_buf, i, t, q):
         parts = convolve(wb, r_buf, i, q)
@@ -605,9 +589,9 @@
             fg[t, :, 128 * z:128 * z + 128] = jnp.where(on > 0.5, parts[h], 0.0).astype(BF)
 
     sweep(bank2, 0, 2, backward)
-    reduce_step()
+    reduce_step(0, 1, 2)
     sweep(bank2, 2, 4, backward)
-    reduce_step()
+    reduce_step(0, 1, 2)
     loads["native"].wait()
     for q in range(4):
         rows = dot(fg[:, :, 256 * q:256 * q + 256].reshape(512, 256), p_native[...])
@@ -615,11 +599,7 @@
     feat_out = pltpu.make_async_copy(feat_v, feat_grad, out_sem.at[0])
     feat_out.start()
 
-    for p in range(3):
-        arrived(reduced[5][p])
-    wd_v[...] = fin[960:1472, :].astype(F32)
-    down_out = pltpu.make_async_copy(wd_v, wd_out, out_sem.at[2])
-    down_out.start()
+    arrived(reduced[0][5] + reduced[1][5])
     for a in range(3):
         for c in range(3):
             for b in range(2):
@@ -630,6 +610,10 @@
             ws_v[9 * a + 6 + c] = fin[rows, column:column + 64].astype(F32)
     sub_out = pltpu.make_async_copy(ws_v, ws_out, out_sem.at[3])
     sub_out.start()
+    arrived(reduced[2][5])
+    wd_v[...] = fin[1024:1536, :].astype(F32)
+    down_out = pltpu.make_async_copy(wd_v, wd_out, out_sem.at[2])
+    down_out.start()
     for copy in halo + halo2 + [dest_send, cg_send, bl_send]:
         copy.wait_send()
     for stage in reduced:
@@ -640,6 +624,15 @@
         copy.wait()
 
 
+def write_out(*refs):
+    sources, targets, sems = refs[:4], refs[4:8], refs[8]
+    copies = [pltpu.make_async_copy(a, b, sems.at[n]) for n, (a, b) in enumerate(zip(sources, targets))]
+    for copy in copies:
+        copy.start()
+    for copy in copies:
+        copy.wait()
+
+
 def shards(features, occupancy, neighbors, coarse_dest, w_sub, w_down, coarse_grad):
     devices = lax.axis_size("gz") * lax.axis_size("gy")
     scale = (features.shape[0] * devices * 512.0) ** -0.5
@@ -647,7 +640,7 @@
     constants = permutations()
     vmem, smem, dma = pltpu.VMEM, pltpu.SMEM, pltpu.SemaphoreType.DMA
     i32 = jnp.int32
-    coarse, feat_grad, ws, wd = pl.pallas_call(
+    held = pl.pallas_call(
         functools.partial(body, scale),
         out_shape=(
             vmem((8, 128, 512), BF), vmem((8, 64, 512), BF), vmem((27, 64, 64), F32), vmem((512, 128), F32),
@@ -686,6 +679,15 @@
         neighbors, occupancy, features, coarse_dest.reshape(1, 8), w_sub,
         w_down.transpose(0, 2, 1), coarse_grad, *constants,
     )
+    coarse, feat_grad, ws, wd = pl.pallas_call(
+        write_out,
+        out_shape=[jax.ShapeDtypeStruct(x.shape, x.dtype) for x in held],
+        in_specs=[anywhere] * 4,
+        out_specs=[anywhere] * 4,
+        scratch_shapes=[dma((4,))],
+        compiler_params=pltpu.CompilerParams(vmem_limit_bytes=1024 * 1024),
+        name="write_out",
+    )(*held)
     return coarse, feat_grad, ws, wd.reshape(8, 64, 128).transpose(0, 2, 1)
 
 

time: 51.8 us -> 48.8 us (0.942)
  local copies, waits for them, and re-layouts: 3.38 us -> 0 us
    unnamed x4 -> x0, local copies, waits for them, and re-layouts: 3.38 us -> none
    pallas_call x0 -> x1, Pallas kernels: none -> 1.55 us  [shards(): pl.pallas_call(write_out, out_shape=[jax.ShapeDtypeStruct(x.shape, x.dtyp...]
    pallas_call x1, Pallas kernels: 47.7 us -> 46.4 us  [shards(): pl.pallas_call(functools.partial(body, scale), out_shape=(vmem((8, 128, 5...]
where the time goes in v3:
time: 48.8 us; the launch traced here: 48.7 us
  Pallas kernels  47.9 us (98%)
  between operations  0.8 us (2%)
    pallas_call x1, Pallas kernels, shards(): pl.pallas_call(functools.partial(body, scale), out_shape=(vmem((8, 128, 5...  46.4 us
    pallas_call x1, Pallas kernels, shards(): pl.pallas_call(write_out, out_shape=[jax.ShapeDtypeStruct(x.shape, x.dtyp...  1.55 us

profile of v3, /device:TPU:1, one launch (start us, length us, event | category | flops | bytes accessed | tf_op | source)
XLA Modules:
  0.0 48.7 jit_solution(5478031523185959159)
XLA Ops:
  0.6 46.4 %sparse_conv.1 = (bf16[8,128,512]{2,1,0:T(8,128)(2,1)S(1)}, bf16[8,64,512]{2,1,0:T(8,128)(2,1)S(1)}, f32[27,64,64]{2,1,0:T(8,128)S(1)}, f32[512,128]{1,0:T(8,128)S(1)}) custom-call(s32[8,27]{1,0:T(8,128)} %refs_0_.1, s32[8,512]{1,0:T(8,128)} %refs_1_.1, bf16[8,64,512]{2,1,0:T(8,128)(2,1)} %refs_2_.1, s32[1,8]{1,0:T(1,128)} %bitcast.7, ...), custom_call_target="tpu_custom_call" | custom-call | flops 6000000000 | bytes 12000000 | tf_op jit(solution)/shard_map/sparse_conv/pallas_call | solution.py:643
  47.0 1.5 %write_out.1 = (bf16[8,128,512]{2,1,0:T(8,128)(2,1)}, bf16[8,64,512]{2,1,0:T(8,128)(2,1)}, f32[27,64,64]{2,1,0:T(8,128)}, f32[512,128]{1,0:T(8,128)}) custom-call(bf16[8,128,512]{2,1,0:T(8,128)(2,1)S(1)} %get-tuple-element.12.refs_0_, bf16[8,64,512]{2,1,0:T(8,128)(2,1)S(1)} %get-tuple-element.13.refs_1_, f32[27,64,64]{2,1,0:T(8,128)S(1)} %get-tuple-element.14.refs_2_, ...), custom_call_target="tpu_custom_call" | custom-call | tf_op jit(solution)/shard_map/write_out/pallas_call | solution.py:682

commit v4 on v3

--- a/solution.py
+++ b/solution.py
@@ -12,7 +12,7 @@
 BF = jnp.bfloat16
 F32 = jnp.float32
 
-Y_LOW, Y_HIGH, ZERO, Z_LOW, Z_HIGH, DIAGONAL, BANK = 64, 128, 192, 200, 208, 216, 248
+Y_SIDES, ZERO, Z_LOW, Z_HIGH, DIAGONAL, BANK = 64, 128, 136, 144, 152, 168
 
 
 def one_hot(shape, pairs):
@@ -43,11 +43,8 @@
         for side in range(2) for z in range(8) for x in range(8)
     ]
     unpack = [
-        [
-            (64 * parity + 8 * z + (xp - 1) % 8, 1024 * parity + 128 * z + 90 * side + xp)
-            for parity in range(2) for z in range(8) for xp in range(10)
-        ]
-        for side in range(2)
+        (128 * side + 64 * parity + 8 * z + (xp - 1) % 8, 1024 * parity + 128 * z + 90 * side + xp)
+        for side in range(2) for parity in range(2) for z in range(8) for xp in range(10)
     ]
     phase, octant = [], []
     for z in range(8):
@@ -65,8 +62,7 @@
         one_hot((128, 128), rewrap),
         one_hot((256, 128), native),
         one_hot((1024, 128), pack),
-        one_hot((128, 2048), unpack[0]),
-        one_hot((128, 2048), unpack[1]),
+        one_hot((256, 2048), unpack),
         one_hot((1024, 512), phase),
         one_hot((512, 1024), flip(phase)),
         one_hot((512, 512), octant),
@@ -86,22 +82,22 @@
     return pltpu.roll(x, shift % 128, x.ndim - 1)
 
 
-PERMUTATIONS = ("wrap", "rewrap", "native", "pack", "un0", "un1", "phase", "unphase", "oct", "unoct")
+PERMUTATIONS = ("wrap", "rewrap", "native", "pack", "unpack", "phase", "unphase", "oct", "unoct")
 
 
 def body(scale, *refs):
-    operands, results, scratch = refs[:17], refs[17:21], refs[21:]
+    operands, results, scratch = refs[:16], refs[16:20], refs[20:]
     nbr_h, occ_h, feat_h, dest_h, w_sub_h, w_down_h, cgrad = operands[:7]
     coarse, feat_grad, ws_out, wd_out = results
     nbr, occ, feat, dest_v, dest_s, w_sub, w_down = scratch[:7]
-    p_wrap, p_rewrap, p_native, p_pack, p_un0, p_un1, p_phase, p_unphase, p_oct, p_unoct = scratch[7:17]
+    p_wrap, p_rewrap, p_native, p_pack, p_unpack, p_phase, p_unphase, p_oct, p_unoct = scratch[7:16]
     (
         bank1, bank2, ysend, ydst, zsend, dsend, drecv, idx_v, idx_s, inv_v, inv_s, dest_buf, dest_in,
         cg_bank, og_in, og_all, og, ag_ph, ag, occ_p, r0, r1, act, phases, pg, wf, wb, wd, wdt,
         bl, bl_in, bl_bank, fg, wg, coarse_v, feat_v, ws_v,
         src, rc, s1, t1, t2, t3, fin, wd_v,
         h_send, h_recv, c_send, c_recv, in_sem, idx_sem, out_sem, r_send, r_recv,
-    ) = scratch[17:]
+    ) = scratch[16:]
     gz, gy = lax.axis_index("gz"), lax.axis_index("gy")
     cy, cz, core = gz // 8, (gz // 2) % 4, gz % 2
     nz, ny = 32, 4
@@ -131,7 +127,7 @@
         loads[name] = pltpu.make_async_copy(source, target, in_sem.at[len(loads)])
         loads[name].start()
 
-    permuting = dict(zip(PERMUTATIONS, zip(operands[7:], scratch[7:17])))
+    permuting = dict(zip(PERMUTATIONS, zip(operands[7:], scratch[7:16])))
     load("feat", feat_h, feat)
     load("occ", occ_h, occ)
     load("wrap", *permuting["wrap"])
@@ -142,7 +138,7 @@
     load("w_sub", w_sub_h, w_sub)
     load("w_down", w_down_h, w_down)
     load("cgrad", cgrad, cg_bank.at[pl.ds(0, 8)])
-    for name in ("unoct", "unphase", "un0", "un1", "rewrap", "phase", "native", "oct"):
+    for name in ("unoct", "unphase", "unpack", "rewrap", "phase", "native", "oct"):
         load(name, *permuting[name])
 
     def send(src, dst, send_sem, recv_sem, device):
@@ -173,8 +169,8 @@
     part_a = column // 9
     edge_z = jnp.where(part_a == 0, 7, 0)
     on_z = Z_LOW + jnp.where(step_z > 0, 8, 0) + slot
-    on_diagonal = DIAGONAL + jnp.where(step_z > 0, 16, 0) + jnp.where(step_y > 0, 8, 0) + slot
-    same_z = jnp.where(step_y == 0, 0, jnp.where(step_y < 0, Y_LOW, Y_HIGH)) + slot * 8 + edge_z
+    on_diagonal = DIAGONAL + jnp.where(step_z > 0, 8, 0) + slot
+    same_z = jnp.where(step_y == 0, 0, Y_SIDES) + slot * 8 + edge_z
     index = jnp.where(step_z == 0, same_z, jnp.where(step_y == 0, on_z, on_diagonal))
     index = jnp.where((table < 0) | ((part_a == 1) & (index > ZERO)), ZERO, index)
     idx_v[...] = jnp.zeros_like(idx_v)
@@ -264,22 +260,20 @@
     def receive(bank, which, copies):
         for copy in copies:
             copy.wait_recv()
-        for side in range(2):
-            rows = ydst[which, side].reshape(256, 128)
-            for q in range(8):
-                planes = dot(rows, (p_un0, p_un1)[side][:, 256 * q:256 * q + 256]).astype(BF)
-                for j in range(4):
-                    for h in range(2):
-                        t, z = 2 * j + q // 4, 2 * (q % 4) + h
-                        bank[(Y_LOW, Y_HIGH)[side] + 8 * t + z] = planes[
-                            64 * j:64 * j + 64, 128 * h:128 * h + 128
-                        ]
+        rows = jnp.concatenate([ydst[which, side].reshape(256, 128) for side in range(2)], axis=1)
+        for q in range(8):
+            planes = dot(rows, p_unpack[:, 256 * q:256 * q + 256]).astype(BF)
+            for j in range(4):
+                for h in range(2):
+                    t, z = 2 * j + q // 4, 2 * (q % 4) + h
+                    bank[Y_SIDES + 8 * t + z] = planes[64 * j:64 * j + 64, 128 * h:128 * h + 128]
         for side_z in range(2):
-            for side_y in range(2):
-                number = 2 * side_z + side_y
-                packed = drecv[which, number].astype(F32)
-                for t in range(8):
-                    bank[DIAGONAL + 8 * number + t] = roll(packed, 90 * side_y - 16 * t).astype(BF)
+            below = drecv[which, 2 * side_z].astype(F32)
+            above = drecv[which, 2 * side_z + 1].astype(F32)
+            for t in range(8):
+                bank[DIAGONAL + 8 * side_z + t] = jnp.where(
+                    yp_low, roll(below, -16 * t), roll(above, 90 - 16 * t)
+                ).astype(BF)
 
     def assemble(bank, t, r_buf, i, planes):
         for zp in planes:
@@ -406,8 +400,7 @@
     inv_copy = pltpu.make_async_copy(inv_v, inv_s, idx_sem.at[3])
     inv_copy.start()
 
-    loads["un0"].wait()
-    loads["un1"].wait()
+    loads["unpack"].wait()
     receive(bank1, 0, halo)
 
     def forward(r_buf, i, t, q):
@@ -429,10 +422,10 @@
     @pl.loop(0, 4)
     def _(i):
         for h in range(2):
-            planes = [pg[8 * (2 * i + h) + z].astype(F32) for z in range(8)]
+            planes = [pg[8 * (2 * i + h) + z] for z in range(8)]
             shifted = jnp.concatenate(
                 [
-                    jnp.concatenate([roll(p, c - 1).astype(BF) for p in planes], axis=1)
+                    jnp.concatenate([roll(p, c - 1) for p in planes], axis=1)
                     for c in range(3)
                 ],
                 axis=0,
@@ -645,7 +638,7 @@
         out_shape=(
             vmem((8, 128, 512), BF), vmem((8, 64, 512), BF), vmem((27, 64, 64), F32), vmem((512, 128), F32),
         ),
-        in_specs=[anywhere] * 17,
+        in_specs=[anywhere] * 16,
         out_specs=(anywhere,) * 4,
         scratch_shapes=[
             vmem((8, 27), i32), vmem((8, 512), i32), vmem((8, 64, 512), BF), vmem((1, 8), i32),

time: 48.8 us -> 48.3 us (0.990)
  Pallas kernels: 47.9 us -> 47.4 us
    pallas_call x1, Pallas kernels: 46.4 us -> 45.9 us  [shards(): pl.pallas_call(functools.partial(body, scale), out_shape=(vmem((8, 128, 5...]
where the time goes in v4:
time: 48.3 us; the launch traced here: 48.2 us
  Pallas kernels  47.4 us (98%)
  between operations  0.8 us (2%)
    pallas_call x1, Pallas kernels, shards(): pl.pallas_call(functools.partial(body, scale), out_shape=(vmem((8, 128, 5...  45.9 us
    pallas_call x1, Pallas kernels, shards(): pl.pallas_call(write_out, out_shape=[jax.ShapeDtypeStruct(x.shape, x.dtyp...  1.55 us

profile of v4, /device:TPU:1, one launch (start us, length us, event | category | flops | bytes accessed | tf_op | source)
XLA Modules:
  0.0 48.2 jit_solution(5936733298601901961)
XLA Ops:
  0.6 45.9 %sparse_conv.1 = (bf16[8,128,512]{2,1,0:T(8,128)(2,1)S(1)}, bf16[8,64,512]{2,1,0:T(8,128)(2,1)S(1)}, f32[27,64,64]{2,1,0:T(8,128)S(1)}, f32[512,128]{1,0:T(8,128)S(1)}) custom-call(s32[8,27]{1,0:T(8,128)} %refs_0_.1, s32[8,512]{1,0:T(8,128)} %refs_1_.1, bf16[8,64,512]{2,1,0:T(8,128)(2,1)} %refs_2_.1, s32[1,8]{1,0:T(1,128)} %bitcast.7, ...), custom_call_target="tpu_custom_call" | custom-call | flops 6000000000 | bytes 12000000 | tf_op jit(solution)/shard_map/sparse_conv/pallas_call | solution.py:636
  46.5 1.5 %write_out.1 = (bf16[8,128,512]{2,1,0:T(8,128)(2,1)}, bf16[8,64,512]{2,1,0:T(8,128)(2,1)}, f32[27,64,64]{2,1,0:T(8,128)}, f32[512,128]{1,0:T(8,128)}) custom-call(bf16[8,128,512]{2,1,0:T(8,128)(2,1)S(1)} %get-tuple-element.12.refs_0_, bf16[8,64,512]{2,1,0:T(8,128)(2,1)S(1)} %get-tuple-element.13.refs_1_, f32[27,64,64]{2,1,0:T(8,128)S(1)} %get-tuple-element.14.refs_2_, ...), custom_call_target="tpu_custom_call" | custom-call | tf_op jit(solution)/shard_map/write_out/pallas_call | solution.py:675

commit v5 on v4

--- a/solution.py
+++ b/solution.py
@@ -241,13 +241,12 @@
         for side_z in range(2):
             for side_y in range(2):
                 number = 2 * side_z + side_y
-                gathered = None
+                gathered = jnp.zeros((64, 128), BF)
                 for t in range(8):
-                    piece = bank[8 * t + (7 if side_z == 0 else 0)].astype(F32)
-                    piece = roll(piece, 16 * t - 90 * side_y)
-                    piece = jnp.where((lanes >= 16 * t) & (lanes < 16 * t + 10), piece, 0.0)
-                    gathered = piece if gathered is None else gathered + piece
-                dsend[which, number] = gathered.astype(BF)
+                    piece = roll(bank[8 * t + (7 if side_z == 0 else 0)], 16 * t - 90 * side_y)
+                    inside = (lanes >= 16 * t) & (lanes < 16 * t + 10)
+                    gathered = jnp.where(inside, piece, gathered)
+                dsend[which, number] = gathered
                 copies.append(
                     send(
                         dsend.at[which, number], drecv.at[which, number],
@@ -268,12 +267,11 @@
                     t, z = 2 * j + q // 4, 2 * (q % 4) + h
                     bank[Y_SIDES + 8 * t + z] = planes[64 * j:64 * j + 64, 128 * h:128 * h + 128]
         for side_z in range(2):
-            below = drecv[which, 2 * side_z].astype(F32)
-            above = drecv[which, 2 * side_z + 1].astype(F32)
+            below, above = drecv[which, 2 * side_z], drecv[which, 2 * side_z + 1]
             for t in range(8):
                 bank[DIAGONAL + 8 * side_z + t] = jnp.where(
                     yp_low, roll(below, -16 * t), roll(above, 90 - 16 * t)
-                ).astype(BF)
+                )
 
     def assemble(bank, t, r_buf, i, planes):
         for zp in planes:
@@ -522,19 +520,15 @@
 
     loads["phase"].wait()
     for q in range(2):
-        split = dot(act[...].reshape(512, 1024), p_phase[:, 256 * q:256 * q + 256])
+        split = dot(act[...].reshape(512, 1024), p_phase[:, 256 * q:256 * q + 256]).astype(BF)
         for j in range(4):
             for h in range(2):
                 even = split[128 * j:128 * j + 64, 128 * h:128 * h + 128]
                 odd = split[128 * j + 64:128 * j + 128, 128 * h:128 * h + 128]
                 k = 4 * q + 2 * h
                 columns = slice(128 * j, 128 * j + 128)
-                phases[64 * k:64 * k + 64, columns] = jnp.where(
-                    low64, even, roll(odd, 64)
-                ).astype(BF)
-                phases[64 * k + 64:64 * k + 128, columns] = jnp.where(
-                    low64, roll(even, 64), odd
-                ).astype(BF)
+                phases[64 * k:64 * k + 64, columns] = jnp.where(low64, even, roll(odd, 64))
+                phases[64 * k + 64:64 * k + 128, columns] = jnp.where(low64, roll(even, 64), odd)
     src[1024:1536, :] = dot_nt(phases[...], og[...])
 
     reduce_step(0, 1, 2)

time: 48.3 us -> 48.7 us (level)
  no operation moved by 1% of the time
where the time goes in v5:
time: 48.7 us; the launch traced here: 48.6 us
  Pallas kernels  47.8 us (98%)
  between operations  0.8 us (2%)
    pallas_call x1, Pallas kernels, shards(): pl.pallas_call(functools.partial(body, scale), out_shape=(vmem((8, 128, 5...  46.3 us
    pallas_call x1, Pallas kernels, shards(): pl.pallas_call(write_out, out_shape=[jax.ShapeDtypeStruct(x.shape, x.dtyp...  1.55 us

profile of v5, /device:TPU:1, one launch (start us, length us, event | category | flops | bytes accessed | tf_op | source)
XLA Modules:
  0.0 48.6 jit_solution(4899604616021965806)
XLA Ops:
  0.6 46.3 %sparse_conv.1 = (bf16[8,128,512]{2,1,0:T(8,128)(2,1)S(1)}, bf16[8,64,512]{2,1,0:T(8,128)(2,1)S(1)}, f32[27,64,64]{2,1,0:T(8,128)S(1)}, f32[512,128]{1,0:T(8,128)S(1)}) custom-call(s32[8,27]{1,0:T(8,128)} %refs_0_.1, s32[8,512]{1,0:T(8,128)} %refs_1_.1, bf16[8,64,512]{2,1,0:T(8,128)(2,1)} %refs_2_.1, s32[1,8]{1,0:T(1,128)} %bitcast.7, ...), custom_call_target="tpu_custom_call" | custom-call | flops 6000000000 | bytes 12000000 | tf_op jit(solution)/shard_map/sparse_conv/pallas_call | solution.py:630
  46.9 1.5 %write_out.1 = (bf16[8,128,512]{2,1,0:T(8,128)(2,1)}, bf16[8,64,512]{2,1,0:T(8,128)(2,1)}, f32[27,64,64]{2,1,0:T(8,128)}, f32[512,128]{1,0:T(8,128)}) custom-call(bf16[8,128,512]{2,1,0:T(8,128)(2,1)S(1)} %get-tuple-element.12.refs_0_, bf16[8,64,512]{2,1,0:T(8,128)(2,1)S(1)} %get-tuple-element.13.refs_1_, f32[27,64,64]{2,1,0:T(8,128)S(1)} %get-tuple-element.14.refs_2_, ...), custom_call_target="tpu_custom_call" | custom-call | tf_op jit(solution)/shard_map/write_out/pallas_call | solution.py:669

commit v6 on v4

--- a/solution.py
+++ b/solution.py
@@ -286,11 +286,10 @@
                     loaded.append(bank[place])
                 rows.append(jnp.where(first, loaded[0], jnp.where(last, loaded[2], loaded[1])))
             plane = jnp.where(yp_low, rows[0], jnp.where(yp_high, rows[2], rows[1]))
-            wide = plane.astype(F32)
             columns = slice(128 * zp, 128 * zp + 128)
-            r_buf[i, 0:64, columns] = roll(wide, 10).astype(BF)
+            r_buf[i, 0:64, columns] = roll(plane, 10)
             r_buf[i, 64:128, columns] = plane
-            r_buf[i, 128:192, columns] = roll(wide, -10).astype(BF)
+            r_buf[i, 128:192, columns] = roll(plane, -10)
 
     def convolve(weights, r_buf, i, q):
         total = None

time: 48.3 us -> 48.4 us (level)
  no operation moved by 1% of the time
where the time goes in v6:
time: 48.4 us; the launch traced here: 48.3 us
  Pallas kernels  47.5 us (98%)
  between operations  0.8 us (2%)
    pallas_call x1, Pallas kernels, shards(): pl.pallas_call(functools.partial(body, scale), out_shape=(vmem((8, 128, 5...  45.9 us
    pallas_call x1, Pallas kernels, shards(): pl.pallas_call(write_out, out_shape=[jax.ShapeDtypeStruct(x.shape, x.dtyp...  1.55 us

profile of v6, /device:TPU:1, one launch (start us, length us, event | category | flops | bytes accessed | tf_op | source)
XLA Modules:
  0.0 48.3 jit_solution(4521563282603997215)
XLA Ops:
  0.6 45.9 %sparse_conv.1 = (bf16[8,128,512]{2,1,0:T(8,128)(2,1)S(1)}, bf16[8,64,512]{2,1,0:T(8,128)(2,1)S(1)}, f32[27,64,64]{2,1,0:T(8,128)S(1)}, f32[512,128]{1,0:T(8,128)S(1)}) custom-call(s32[8,27]{1,0:T(8,128)} %refs_0_.1, s32[8,512]{1,0:T(8,128)} %refs_1_.1, bf16[8,64,512]{2,1,0:T(8,128)(2,1)} %refs_2_.1, s32[1,8]{1,0:T(1,128)} %bitcast.7, ...), custom_call_target="tpu_custom_call" | custom-call | flops 6000000000 | bytes 12000000 | tf_op jit(solution)/shard_map/sparse_conv/pallas_call | solution.py:635
  46.6 1.5 %write_out.1 = (bf16[8,128,512]{2,1,0:T(8,128)(2,1)}, bf16[8,64,512]{2,1,0:T(8,128)(2,1)}, f32[27,64,64]{2,1,0:T(8,128)}, f32[512,128]{1,0:T(8,128)}) custom-call(bf16[8,128,512]{2,1,0:T(8,128)(2,1)S(1)} %get-tuple-element.12.refs_0_, bf16[8,64,512]{2,1,0:T(8,128)(2,1)S(1)} %get-tuple-element.13.refs_1_, f32[27,64,64]{2,1,0:T(8,128)S(1)} %get-tuple-element.14.refs_2_, ...), custom_call_target="tpu_custom_call" | custom-call | tf_op jit(solution)/shard_map/write_out/pallas_call | solution.py:674
